TPU v7x, 512 devices: a whole 4x4x16 slice. The times are simulated.
512 devices in a mesh: row: 32 (over y_lo, z), col: 16 (over y_hi, x, core).
Axes of the slice: x: 4, y: 4 (y_hi: 2, y_lo: 2; y = y_hi * 2 + y_lo), z: 16, core: 2. Of those that a mesh axis runs over, the one named last changes fastest.
Arguments:
- features: bfloat16 [16, 32, 256, 128], P('col', 'row'), may hold values from -6 to 6
- weight: bfloat16 [128, 256], replicated, may hold values from -0.5 to 0.5
- tile_values: bfloat16 [32, 16, 128, 128, 128], P('row', 'col'), may hold values from -0.125 to 0.125
- tile_rows: int32 [32, 16, 128], P('row', 'col'), may hold values from 0 to 31
- tile_cols: int32 [32, 16, 128], P('row', 'col'), may hold values from 0 to 63
- tile_count: int32 [32, 16], P('row', 'col'), may hold values from 1 to 128, as said below
- cotangent: bfloat16 [131072, 256], P(('row', 'col')), may hold values from -6 to 6
Outputs:
- activations: bfloat16 [131072, 256], P(('row', 'col'))
- weight_grad: float32 [128, 256], replicated
- feature_grad: float32 [16, 32, 256, 128], P('col', 'row')
Inputs may be any that keep to these rules, and one draw needn't show every extreme that they name: `tile_count`: the slots in use of each block; at least one block uses all 128.
All inputs are finite; a program needn't handle non-finite values.
Results may differ from a plain program's by a relative error of at most 0.03.
Values may be sent and summed in bfloat16 or wider, within the bound.
No kernel may reach another device: no remote copies, remote signals or barrier semaphores. Data moves between devices by JAX's collectives and lax.ppermute only.
A program may use at most 64 MiB of HBM per device.

v0:
```python
import math

import jax
import jax.numpy as jnp
from jax import lax
from jax.sharding import PartitionSpec as P


def on_device(features, weight, tile_values, tile_rows, tile_cols, tile_count, cotangent):
    sub_rows = features.shape[2]
    width = features.shape[3]
    slots = tile_values.shape[2]
    tile = tile_values.shape[3]
    n_row = lax.axis_size("row")
    n_col = lax.axis_size("col")
    tile_rows_n = n_col * sub_rows // tile
    tile_cols_n = n_row * sub_rows // tile
    live = jnp.arange(slots, dtype=jnp.int32) < tile_count[0, 0]
    values = jnp.where(live[:, None, None], tile_values[0, 0], jnp.zeros((), jnp.bfloat16))
    rows = tile_rows[0, 0]
    cols = tile_cols[0, 0]
    onehot_rows = (rows[:, None] == jnp.arange(tile_rows_n, dtype=jnp.int32)[None, :]).astype(
        jnp.float32
    )
    onehot_cols = (cols[:, None] == jnp.arange(tile_cols_n, dtype=jnp.int32)[None, :]).astype(
        jnp.float32
    )
    colblock = lax.all_gather(features[0, 0], "row", axis=0, tiled=True)
    picked = colblock.reshape(tile_cols_n, tile, width)[cols]
    products = jnp.einsum("sij,sjf->sif", values, picked, preferred_element_type=jnp.float32)
    partial_value = jnp.einsum("st,sif->tif", onehot_rows, products).reshape(
        tile_rows_n * tile, width
    )
    aggregated = lax.psum_scatter(
        partial_value.astype(jnp.bfloat16), "col", scatter_dimension=0, tiled=True
    )
    pre = jnp.dot(aggregated, weight, preferred_element_type=jnp.float32)
    activations = jax.nn.silu(pre).astype(jnp.bfloat16)
    sig = jax.nn.sigmoid(pre)
    grad_pre = (cotangent.astype(jnp.float32) * (sig * (1.0 + pre * (1.0 - sig)))).astype(
        jnp.bfloat16
    )
    local_grad = lax.dot_general(
        aggregated, grad_pre, (((0,), (0,)), ((), ())), preferred_element_type=jnp.float32
    )
    summed = lax.psum(local_grad, ("row", "col"))
    weight_grad = summed * (1.0 / math.sqrt(sub_rows * n_row * n_col))
    back = lax.dot_general(
        grad_pre, weight, (((1,), (1,)), ((), ())), preferred_element_type=jnp.float32
    ).astype(jnp.bfloat16)
    rowblock = lax.all_gather(back, "col", axis=0, tiled=True)
    chosen_rows = rowblock.reshape(tile_rows_n, tile, width)[rows]
    tproducts = jnp.einsum("sij,sif->sjf", values, chosen_rows, preferred_element_type=jnp.float32)
    tpartial = jnp.einsum("st,sjf->tjf", onehot_cols, tproducts).reshape(tile_cols_n * tile, width)
    feature_grad = lax.psum_scatter(
        tpartial.astype(jnp.bfloat16), "row", scatter_dimension=0, tiled=True
    ).astype(jnp.float32)
    return (activations, weight_grad, feature_grad.reshape(1, 1, sub_rows, width))


def solution(mesh):
    in_specs = (
        P("col", "row", None, None),
        P(),
        P("row", "col", None, None, None),
        P("row", "col", None),
        P("row", "col", None),
        P("row", "col"),
        P(("row", "col"), None),
    )
    out_specs = (P(("row", "col"), None), P(), P("col", "row", None, None))
    return jax.shard_map(
        on_device, mesh=mesh, in_specs=in_specs, out_specs=out_specs, check_vma=False
    )
```

profile of v0, /device:TPU:2, one launch (start us, length us, event | category | flops | bytes accessed | tf_op | source)
XLA Modules:
  0.0 902.4 jit_solution(13224221884042204989)
XLA Ops:
  7.2 0.0 copy-start
  7.2 0.0 all-gather.6.cloned.1.call-start
  7.2 0.7 all-gather.6.cloned.1.call-update
  7.9 0.0 reduce-scatter.3.cloned.1.call-start
  8.6 0.7 fusion.18
  9.3 138.9 %all-gather.6.cloned.1.call-done = bf16[1,1,8192,128]{3,2,1,0:T(8,128)(2,1)} async-done(((bf16[1,1,256,128]{3,2,1,0:T(8,128)(2,1)}), bf16[1,1,8192,128]{3,2,1,0:T(8,128)(2,1)}) %all-gather.6.cloned.1.call-update) | async-done | bytes 2097168 | tf_op jit(solution)/shard_map/all_gather | solution.py:28
  148.2 4.6 gather_fusion
  152.8 0.0 copy-start.2
  152.8 4.8 fusion.8
  157.6 0.0 copy-done.2
  157.6 0.0 copy-start.3
  157.6 2.6 fusion.9
  160.3 1.4 copy.10
  161.6 0.0 reduce-scatter.3.cloned.1.call-update
  161.7 0.0 all-gather.4.cloned.1.call-start
  161.7 83.1 %reduce-scatter.3.cloned.1.call-done = bf16[256,128]{1,0:T(8,128)(2,1)} async-done(((bf16[4096,128]{1,0:T(8,128)(2,1)}), bf16[256,128]{1,0:T(8,128)(2,1)}) %reduce-scatter.3.cloned.1.call-update) | async-done | bytes 65552 | tf_op jit(solution)/shard_map/reduce_scatter | solution.py:34
  244.8 0.0 copy-done
  244.8 0.0 copy-done.3
  244.8 1.8 multiply_convert_fusion
  246.5 0.8 convolution_convert_fusion
  247.4 0.0 all-gather.4.cloned.1.call-update
  247.4 0.0 all-reduce.2.cloned.1.call-start
  247.5 1.7 fusion.22
  249.2 0.0 all-reduce.2.cloned.1.call-update
  249.2 0.2 reduce-scatter.5.cloned.1.call-start
  249.4 59.5 %all-gather.4.cloned.1.call-done = bf16[4096,128]{1,0:T(8,128)(2,1)} async-done(((bf16[256,128]{1,0:T(8,128)(2,1)}), bf16[4096,128]{1,0:T(8,128)(2,1)}) %all-gather.4.cloned.1.call-update) | async-done | bytes 1048592 | tf_op jit(solution)/shard_map/all_gather | solution.py:51
  308.9 4.3 gather_fusion.1
  313.2 0.0 copy-start.1
  313.2 5.2 fusion.7
  318.4 0.0 copy-done.1
  318.4 3.0 fusion.4
  321.3 2.7 copy.11
  324.0 0.0 reduce-scatter.5.cloned.1.call-update
  324.0 437.4 %all-reduce.2.cloned.1.call-done = f32[128,256]{1,0:T(8,128)} async-done(((f32[128,256]{1,0:T(8,128)}), f32[128,256]{1,0:T(8,128)}) %all-reduce.2.cloned.1.call-update) | async-done | bytes 131088 | tf_op jit(solution)/shard_map/psum | solution.py:46
  761.4 1.6 broadcast_multiply_fusion
  763.0 131.4 %reduce-scatter.5.cloned.1.call-done = bf16[256,128]{1,0:T(8,128)(2,1)} async-done(((bf16[8192,128]{1,0:T(8,128)(2,1)}), bf16[256,128]{1,0:T(8,128)(2,1)}) %reduce-scatter.5.cloned.1.call-update) | async-done | bytes 65552 | tf_op jit(solution)/shard_map/reduce_scatter | solution.py:55
  894.4 1.5 bitcast_convert_fusion
  (4 shorter events, 0.0 us)
Async XLA Ops:
  7.2 237.6 %copy-start = (bf16[128,256]{1,0:T(8,128)(2,1)S(1)}, bf16[128,256]{1,0:T(8,128)(2,1)}, u32[]{:S(2)}) copy-start(bf16[128,256]{1,0:T(8,128)(2,1)} %param.8) | copy-start | bytes 196612
  7.2 141.0 %all-gather.6.cloned.1.call-start = ((), (), s32[]{:S(2)}) async-start(), calls=%async_computation.6 | async-start | bytes 2162688 | tf_op jit(solution)/shard_map/all_gather | solution.py:28
  7.9 236.9 %reduce-scatter.3.cloned.1.call-start = ((), (), s32[]{:S(2)}) async-start(), calls=%async_computation.2 | async-start | bytes 1114112 | tf_op jit(solution)/shard_map/reduce_scatter | solution.py:34
  152.8 4.8 copy-start.2
  157.6 87.2 %copy-start.3 = (bf16[256,256]{1,0:T(8,128)(2,1)S(1)}, bf16[256,256]{1,0:T(8,128)(2,1)}, u32[]{:S(2)}) copy-start(bf16[256,256]{1,0:T(8,128)(2,1)} %param.13) | copy-start | bytes 393220
  161.7 147.3 %all-gather.4.cloned.1.call-start = ((), (), s32[]{:S(2)}) async-start(), calls=%async_computation.4 | async-start | bytes 1114112 | tf_op jit(solution)/shard_map/all_gather | solution.py:51
  247.4 514.0 %all-reduce.2.cloned.1.call-start = ((), (), s32[]{:S(2)}) async-start(), calls=%async_computation.3 | async-start | bytes 262144 | tf_op jit(solution)/shard_map/psum | solution.py:46
  249.2 645.2 %reduce-scatter.5.cloned.1.call-start = ((), (), s32[]{:S(2)}) async-start(), calls=%async_computation.5 | async-start | bytes 2162688 | tf_op jit(solution)/shard_map/reduce_scatter | solution.py:55
  313.2 5.2 copy-start.1
Sparse Core Ops, SparseCore 0:
  10.1 138.0 all-gather.5
  161.8 82.9 reduce-scatter.2
  249.2 59.6 all-gather.3
  315.7 445.6 all-reduce.1
  764.1 130.3 reduce-scatter.4
where the time goes:
time: 903 us; the launch traced here: 902 us
  waiting for transfers between devices  851 us (94%)
  matrix products  19.8 us (2%)
  between operations  14.5 us (2%)
  local copies, waits for them, and re-layouts  13 us (1%)
    psum x1, waiting for transfers between devices, on_device(): summed = lax.psum(local_grad, ('row', 'col'))  437 us
    all_gather x1, waiting for transfers between devices, on_device(): colblock = lax.all_gather(features[0, 0], 'row', axis=0, tiled=True)  139 us
    reduce_scatter x1, waiting for transfers between devices, on_device(): lax.psum_scatter(tpartial.astype(jnp.bfloat16), 'row', scatter_dimension=...  131 us
    reduce_scatter x1, waiting for transfers between devices, on_device(): lax.psum_scatter(partial_value.astype(jnp.bfloat16), 'col', scatter_dimen...  83.1 us
    all_gather x1, waiting for transfers between devices, on_device(): rowblock = lax.all_gather(back, 'col', axis=0, tiled=True)  59.5 us
  transfers between devices with their start and end apart: 5, of which 5 were waited for; matrix products, arithmetic and copies ran while one was open for 2% of the time, Pallas kernels for 0%

commit v1 on v0

v1 whole, which is shorter than its diff:
```python
import math

import jax
import jax.numpy as jnp
from jax import lax
from jax.experimental import pallas as pl
from jax.experimental.pallas import tpu as pltpu
from jax.sharding import PartitionSpec as P

BF16 = jnp.bfloat16
F32 = jnp.float32
ANY = pl.BlockSpec(memory_space=pl.ANY)
SMEM = pl.BlockSpec(memory_space=pltpu.SMEM)
VMEM = pl.BlockSpec(memory_space=pltpu.VMEM)
VMEM_LIMIT = 32 * 1024 * 1024

N_Y, N_ZH, N_ZL = 2, 4, 4
N_Z = N_ZH * N_ZL
N_PAIR, N_CORE = 8, 2
CHUNK = 16
UNROLL = 4


def shift(x, dy, dz):
    pairs = [
        (y * N_Z + z, (y + dy) % N_Y * N_Z + (z + dz) % N_Z) for y in range(N_Y) for z in range(N_Z)
    ]
    return lax.ppermute(x, "row", pairs)


def swap_cores(x):
    return lax.ppermute(x, "col", [(c, c ^ 1) for c in range(N_PAIR * N_CORE)])


Z_GROUPS = [[y * N_Z + z for z in range(N_Z)] for y in range(N_Y)]
ZH_GROUPS = [
    [y * N_Z + zh * N_ZL + zl for zh in range(N_ZH)] for y in range(N_Y) for zl in range(N_ZL)
]
PAIR_GROUPS = [[p * N_CORE + core for p in range(N_PAIR)] for core in range(N_CORE)]


def exchange(x, axis, groups):
    return lax.all_to_all(x, axis, 0, 0, tiled=True, axis_index_groups=groups)


def copies(x, n):
    return jnp.broadcast_to(x[None], (n,) + x.shape)


def add_up(parts):
    total = parts[0].astype(F32)
    for part in parts[1:]:
        total = total + part.astype(F32)
    return total


def start_tiles(values_hbm, values, sems):
    for c in range(values.shape[0] // CHUNK):
        s = pl.ds(c * CHUNK, CHUNK)
        pltpu.make_async_copy(values_hbm.at[s], values.at[s], sems.at[c]).start()


def each_tile(count, values_hbm, values, sems, step):
    def chunk(c, _):
        s = pl.ds(c * CHUNK, CHUNK)
        pltpu.make_async_copy(values_hbm.at[s], values.at[s], sems.at[c]).wait()
        left = jnp.clip(count - c * CHUNK, 0, CHUNK)

        def body(i, _):
            step(c * CHUNK + i * UNROLL)
            return 0

        lax.fori_loop(0, (left + UNROLL - 1) // UNROLL, body, 0)
        return 0

    lax.fori_loop(0, values.shape[0] // CHUNK, chunk, 0)


def forward_kernel(meta, rows, places, values_hbm, z0, z1, z2, z3, z4, o0, o12, o34, keep, send,
                   values, block, total, value_sems, block_sems):
    start_tiles(values_hbm, values, value_sems)
    q = z0.shape[0]
    moves = [(z0, 0), (z1, q), (z2, 2 * q), (z3, 3 * q), (z4, 3 * q + q // 2), (o0, 4 * q),
             (o12, 5 * q), (o34, 7 * q)]
    moves = [
        pltpu.make_async_copy(src, block.at[pl.ds(at, src.shape[0])], block_sems.at[i])
        for i, (src, at) in enumerate(moves)
    ]
    for move in moves:
        move.start()
    total[...] = jnp.zeros_like(total)
    for move in moves:
        move.wait()
    count = meta[0]
    core = meta[1]
    dump = total.shape[0] - 1

    def step(first):
        products = [
            jnp.dot(values[first + u], block[places[first + u]], preferred_element_type=F32)
            for u in range(UNROLL)
        ]
        for u in range(UNROLL):
            row = jnp.where(first + u < count, rows[first + u], dump)
            total[row] += products[u]

    each_tile(count, values_hbm, values, value_sems, step)
    tile = total.shape[1]
    for p in range(N_PAIR):
        for i in range(2):
            at = pl.ds((2 * p + i) * tile, tile)
            keep[at] = total[(2 * p + core) * 2 + i].astype(BF16)
            send[at] = total[(2 * p + 1 - core) * 2 + i].astype(BF16)


def middle_kernel(parts, weight, cotangent, activations, payload):
    n, sub, width = parts.shape
    aggregated = parts[0].astype(F32)
    for p in range(1, n):
        aggregated = aggregated + parts[p].astype(F32)
    aggregated = aggregated.astype(BF16)
    pre = jnp.dot(aggregated, weight[...], preferred_element_type=F32)
    sig = jax.nn.sigmoid(pre)
    activations[...] = (pre * sig).astype(BF16)
    grad_pre = (cotangent[...].astype(F32) * (sig * (1.0 + pre * (1.0 - sig)))).astype(BF16)
    local = lax.dot_general(
        aggregated, grad_pre, (((0,), (0,)), ((), ())), preferred_element_type=F32
    ).astype(BF16)
    back = lax.dot_general(
        weight[...], grad_pre, (((1,), (1,)), ((), ())), preferred_element_type=F32
    ).astype(BF16)
    share = 2 * width // n
    half = n // 2
    for p in range(n):
        payload[p, :width] = back[:, :width]
        payload[p, width:2 * width] = back[:, width:]
        k = p % half * share
        payload[p, 2 * width:] = local[k:k + share, p // half * width:(p // half + 1) * width]


def backward_kernel(meta, cols, places, values_hbm, mine, other, keep, send,
                    values, block, total, value_sems, block_sems):
    start_tiles(values_hbm, values, value_sems)
    pairs, two = block.shape[1], block.shape[2]
    moves = [
        pltpu.make_async_copy(src.at[:, pl.ds(0, two)], block.at[i], block_sems.at[i])
        for i, src in enumerate((mine, other))
    ]
    for move in moves:
        move.start()
    total[...] = jnp.zeros_like(total)
    for move in moves:
        move.wait()
    count = meta[0]
    my_y = meta[2]
    my_zl = meta[3]
    dump = total.shape[0] - 1
    tile = total.shape[1]

    def step(first):
        products = []
        for u in range(UNROLL):
            at = places[first + u]
            back = block[at // (2 * pairs), at // 2 % pairs, pl.ds(at % 2 * tile, tile)]
            products.append(jnp.dot(back, values[first + u], preferred_element_type=F32))
        for u in range(UNROLL):
            col = jnp.where(first + u < count, cols[first + u], dump)
            total[col] += products[u]

    each_tile(count, values_hbm, values, value_sems, step)
    for d, offset in enumerate((0, 1, 3, 2)):
        zl = (my_zl + offset) % N_ZL
        for zh in range(N_ZH):
            for i in range(2):
                at = pl.ds(((d * N_ZH + zh) * 2 + i) * tile, tile)
                keep[at] = total[(my_y * N_Z + zh * N_ZL + zl) * 2 + i].astype(BF16)
                send[at] = total[((1 - my_y) * N_Z + zh * N_ZL + zl) * 2 + i].astype(BF16)


def on_device(features, weight, tile_values, tile_rows, tile_cols, tile_count, cotangent):
    sub, width = features.shape[2:]
    slots, tile = tile_values.shape[2:4]
    n_row = lax.axis_size("row")
    n_col = lax.axis_size("col")
    assert n_row == N_Y * N_Z and n_col == N_PAIR * N_CORE
    assert tile == width and sub == 2 * tile
    r = lax.axis_index("row")
    c = lax.axis_index("col")
    my_y, my_zl, core = r // N_Z, r % N_ZL, c % N_CORE
    values = tile_values[0, 0]
    rows = tile_rows[0, 0]
    cols = tile_cols[0, 0]
    meta = jnp.stack([tile_count[0, 0], core, my_y, my_zl]).astype(jnp.int32)

    at = cols // 2
    distance = jnp.array([0, 2, 3, 1], jnp.int32)[(at - my_zl) % N_ZL]
    col_places = (
        (((at // N_Z) ^ my_y) * N_ZL + distance) * N_ZH + at // N_ZL % N_ZH
    ) * 2 + cols % 2
    at = rows // 2
    row_places = (((at % N_CORE) ^ core) * N_PAIR + at // N_CORE) * 2 + rows % 2

    z0 = exchange(copies(features[0, 0], N_ZH).reshape(N_ZH * sub, width), "row", ZH_GROUPS)
    half = z0.shape[0] // 2
    z1, z2 = shift(z0, 0, 1), shift(z0, 0, -1)
    z3, z4 = shift(z0[:half], 0, 2), shift(z0[half:], 0, -2)
    o0 = shift(z0, 1, 0)
    o12 = shift(jnp.concatenate([z1, z2]), 1, 0)
    o34 = shift(jnp.concatenate([z3, z4]), 1, 0)
    pieces = [
        piece.reshape(-1, tile, width) for piece in (z0, z1, z2, z3, z4, o0, o12, o34)
    ]
    n_chunks = slots // CHUNK
    rows_n = n_col * sub // tile
    cols_n = n_row * sub // tile
    half_rows = jax.ShapeDtypeStruct((n_col * sub // 2, width), BF16)
    half_cols = jax.ShapeDtypeStruct((n_row * sub // 2, width), BF16)
    flops = 2 * slots * tile * tile * width
    params = pltpu.CompilerParams(vmem_limit_bytes=VMEM_LIMIT)
    keep, send = pl.pallas_call(
        forward_kernel,
        out_shape=(half_rows, half_rows),
        in_specs=[SMEM, SMEM, SMEM] + [ANY] * 9,
        out_specs=(VMEM, VMEM),
        scratch_shapes=[
            pltpu.VMEM((slots, tile, tile), BF16),
            pltpu.VMEM((cols_n, tile, width), BF16),
            pltpu.VMEM((rows_n + 1, tile, width), F32),
            pltpu.SemaphoreType.DMA((n_chunks,)),
            pltpu.SemaphoreType.DMA((len(pieces),)),
        ],
        compiler_params=params,
        cost_estimate=pl.CostEstimate(flops=flops, bytes_accessed=7 << 20, transcendentals=0),
        name="forward_tiles",
    )(meta, rows, col_places, values, *pieces)

    both = (keep.astype(F32) + swap_cores(send).astype(F32)).astype(BF16)
    parts = exchange(both, "col", PAIR_GROUPS).reshape(N_PAIR, sub, width)
    share = 2 * width // N_PAIR
    activations, payload = pl.pallas_call(
        middle_kernel,
        out_shape=(
            jax.ShapeDtypeStruct(cotangent.shape, BF16),
            jax.ShapeDtypeStruct((N_PAIR, sub + share, width), BF16),
        ),
        in_specs=[VMEM] * 3,
        out_specs=(VMEM, VMEM),
        compiler_params=params,
        name="layer",
    )(parts, weight, cotangent)

    mine = exchange(payload.reshape(-1, width), "col", PAIR_GROUPS).reshape(payload.shape)
    other = swap_cores(mine)
    keep, send = pl.pallas_call(
        backward_kernel,
        out_shape=(half_cols, half_cols),
        in_specs=[SMEM, SMEM, SMEM] + [ANY] * 3,
        out_specs=(VMEM, VMEM),
        scratch_shapes=[
            pltpu.VMEM((slots, tile, tile), BF16),
            pltpu.VMEM((N_CORE, N_PAIR, sub, width), BF16),
            pltpu.VMEM((cols_n + 1, tile, width), F32),
            pltpu.SemaphoreType.DMA((n_chunks,)),
            pltpu.SemaphoreType.DMA((N_CORE,)),
        ],
        compiler_params=params,
        cost_estimate=pl.CostEstimate(flops=flops, bytes_accessed=7 << 20, transcendentals=0),
        name="backward_tiles",
    )(meta, cols, row_places, values, mine, other)

    shared = add_up([mine[p, sub:] for p in range(N_PAIR)]) + add_up(
        [other[p, sub:] for p in range(N_PAIR)]
    )
    shared = shared + shift(shared, 1, 0)
    along_z = exchange(copies(shared, N_Z).reshape(-1, width), "row", Z_GROUPS)
    along_z = along_z.reshape(N_Z, share, width)
    shared = add_up([along_z[z] for z in range(N_Z)])
    summed = exchange(copies(shared, N_PAIR).reshape(-1, width), "col", PAIR_GROUPS)
    summed = summed.reshape(2, width, width).transpose(1, 0, 2).reshape(width, 2 * width)
    weight_grad = summed * (1.0 / math.sqrt(sub * n_row * n_col))

    held = (keep.astype(F32) + shift(send, 1, 0).astype(F32)).astype(BF16)
    q = held.shape[0] // N_ZL
    near = shift(held[q:2 * q], 0, 1), shift(held[2 * q:3 * q], 0, -1)
    far = shift(held[3 * q:3 * q + q // 2], 0, 2), shift(held[3 * q + q // 2:], 0, -2)
    held = add_up([held[:q], near[0], near[1], jnp.concatenate(far)]).astype(BF16)
    far = exchange(held, "row", ZH_GROUPS).reshape(N_ZH, 2, width, tile)
    feature_grad = add_up([far[zh] for zh in range(N_ZH)]).transpose(0, 2, 1)
    return activations, weight_grad, feature_grad.reshape(1, 1, sub, width)


def solution(mesh):
    in_specs = (
        P("col", "row", None, None),
        P(),
        P("row", "col", None, None, None),
        P("row", "col", None),
        P("row", "col", None),
        P("row", "col"),
        P(("row", "col"), None),
    )
    out_specs = (P(("row", "col"), None), P(), P("col", "row", None, None))
    return jax.shard_map(
        on_device, mesh=mesh, in_specs=in_specs, out_specs=out_specs, check_vma=False
    )
```

time: 903 us -> 222 us (0.25)
  the two profiles are of different devices: /device:TPU:2 before, /device:TPU:32 now
where the time goes in v1:
time: 222 us; the launch traced here: 221 us
  waiting for transfers between devices  68.9 us (31%)
  blocking collectives  68.4 us (31%)
  starting transfers between devices  65.3 us (29%)
  Pallas kernels  7.75 us (3%)
  local copies, waits for them, and re-layouts  6.18 us (3%)
  other arithmetic  2.76 us (1%)
    all_to_all x3, blocking collectives, exchange(): return lax.all_to_all(x, axis, 0, 0, tiled=True, axis_index_groups=groups)  68.4 us
    ppermute x13, starting transfers between devices, shift(): return lax.ppermute(x, 'row', pairs)  46.6 us
    ppermute x13, waiting for transfers between devices, shift(): return lax.ppermute(x, 'row', pairs)  39.6 us
    all_to_all x3, waiting for transfers between devices, exchange(): return lax.all_to_all(x, axis, 0, 0, tiled=True, axis_index_groups=groups)  25.5 us
    all_to_all x3, starting transfers between devices, exchange(): return lax.all_to_all(x, axis, 0, 0, tiled=True, axis_index_groups=groups)  14.7 us
  transfers between devices with their start and end apart: 18, of which 10 were waited for; matrix products, arithmetic and copies ran while one was open for 2% of the time, Pallas kernels for 0%

profile of v1, /device:TPU:32, one launch (start us, length us, event | category | flops | bytes accessed | tf_op | source)
XLA Modules:
  0.0 220.9 jit_solution(10265134689251820967)
XLA Ops:
  0.7 0.9 broadcast_in_dim.11
  1.5 35.3 %all_to_all.45 = bf16[4,256,128]{2,1,0:T(8,128)(2,1)S(1)} all-to-all(bf16[4,256,128]{2,1,0:T(8,128)(2,1)S(1)} %broadcast_in_dim.11), channel_id=1, replica_groups={{0,64,128,192},{16,80,144,208},{32,96,160,224},{48,112,176,240},{256,32..., dimensions={0} | all-to-all | bytes 524288 | tf_op jit(solution)/shard_map/all_to_all | solution.py:43
  36.8 1.9 collective-permute-start.1
  38.7 3.9 %collective-permute-start = (bf16[1024,128]{1,0:T(8,128)(2,1)S(1)}, bf16[1024,128]{1,0:T(8,128)(2,1)S(1)}, u32[]{:S(2)}, u32[]{:S(2)}) collective-permute-start(bf16[1024,128]{1,0:T(8,128)(2,1)S(1)} %bitcast.55), channel_id=1, source_target_pairs={{0,16},{16,32},{32,48},{48,64},{64,80},{80,96},{96,112},{112,128},... | collective-permute-start | bytes 786440 | tf_op jit(solution)/shard_map/ppermute | solution.py:28
  42.7 2.5 %collective-permute-start.2 = (bf16[512,128]{1,0:T(8,128)(2,1)S(1)}, bf16[512,128]{1,0:T(8,128)(2,1)S(1)}, u32[]{:S(2)}, u32[]{:S(2)}) collective-permute-start(bf16[512,128]{1,0:T(8,128)(2,1)S(1)} %bitcast.73), channel_id=1, source_target_pairs={{0,32},{16,48},{32,64},{48,80},{64,96},{80,112},{96,128},{112,144}... | collective-permute-start | bytes 393224 | tf_op jit(solution)/shard_map/ppermute | solution.py:28
  45.1 5.5 %collective-permute-start.3 = (bf16[512,128]{1,0:T(8,128)(2,1)S(1)}, bf16[512,128]{1,0:T(8,128)(2,1)S(1)}, u32[]{:S(2)}, u32[]{:S(2)}) collective-permute-start(bf16[512,128]{1,0:T(8,128)(2,1)S(1)} %bitcast.72), channel_id=1, source_target_pairs={{0,224},{16,240},{32,0},{48,16},{64,32},{80,48},{96,64},{112,80},{... | collective-permute-start | bytes 393224 | tf_op jit(solution)/shard_map/ppermute | solution.py:28
  50.6 0.0 collective-permute-done.1
  50.7 0.3 collective-permute-done
  51.0 3.5 %collective-permute-start.5 = (bf16[2048,128]{1,0:T(8,128)(2,1)S(1)}, bf16[2048,128]{1,0:T(8,128)(2,1)S(1)}, u32[]{:S(2)}, u32[]{:S(2)}) collective-permute-start(bf16[2048,128]{1,0:T(8,128)(2,1)S(1)} %pad_maximum_fusion), channel_id=1, source_target_pairs={{0,256},{16,272},{32,288},{48,304},{64,320},{80,336},{96,352},{112... | collective-permute-start | bytes 1572872 | tf_op jit(solution)/shard_map/ppermute | solution.py:28
  55.1 2.4 %collective-permute-start.4 = (bf16[1024,128]{1,0:T(8,128)(2,1)S(1)}, bf16[1024,128]{1,0:T(8,128)(2,1)S(1)}, u32[]{:S(2)}, u32[]{:S(2)}) collective-permute-start(bf16[1024,128]{1,0:T(8,128)(2,1)S(1)} %bitcast.56), channel_id=1, source_target_pairs={{0,256},{16,272},{32,288},{48,304},{64,320},{80,336},{96,352},{112... | collective-permute-start | bytes 786440 | tf_op jit(solution)/shard_map/ppermute | solution.py:28
  57.6 3.5 %collective-permute-start.6 = (bf16[1024,128]{1,0:T(8,128)(2,1)S(1)}, bf16[1024,128]{1,0:T(8,128)(2,1)S(1)}, u32[]{:S(2)}, u32[]{:S(2)}) collective-permute-start(bf16[1024,128]{1,0:T(8,128)(2,1)S(1)} %pad_maximum_fusion.1), channel_id=1, source_target_pairs={{0,256},{16,272},{32,288},{48,304},{64,320},{80,336},{96,352},{112... | collective-permute-start | bytes 786440 | tf_op jit(solution)/shard_map/ppermute | solution.py:28
  61.1 0.1 pad_add_fusion.meta
  61.2 11.2 %collective-permute-done.4 = bf16[1024,128]{1,0:T(8,128)(2,1)S(1)} collective-permute-done((bf16[1024,128]{1,0:T(8,128)(2,1)S(1)}, bf16[1024,128]{1,0:T(8,128)(2,1)S(1)}, u32[]{:S(2)}, u32[]{:S(2)}) %collective-permute-start.4) | collective-permute-done | bytes 262176 | tf_op jit(solution)/shard_map/ppermute | solution.py:28
  72.4 2.8 %collective-permute-done.6 = bf16[1024,128]{1,0:T(8,128)(2,1)S(1)} collective-permute-done((bf16[1024,128]{1,0:T(8,128)(2,1)S(1)}, bf16[1024,128]{1,0:T(8,128)(2,1)S(1)}, u32[]{:S(2)}, u32[]{:S(2)}) %collective-permute-start.6) | collective-permute-done | bytes 262176 | tf_op jit(solution)/shard_map/ppermute | solution.py:28
  75.2 2.2 copy-done
  77.4 3.5 %forward_tiles.1 = (bf16[2048,128]{1,0:T(8,128)(2,1)S(1)}, bf16[2048,128]{1,0:T(8,128)(2,1)S(1)}) custom-call(s32[4]{0:T(128)S(1)} %pad_add_fusion.meta, s32[128]{0:T(128)S(1)} %bitcast.66, s32[128]{0:T(128)S(1)} %fusion.2.places, bf16[128,128,128]{2,1,0:T(8,128)(2,1)S(1)} %bitcast.52, bf16[8,128,128]{2,1,0:T(8,128)(2,1)S(1)} %bitcast.57, ...), custom_call_target="tpu_custom_call" | custom-call | flops 536870912 | bytes 7340032 | tf_op jit(solution)/shard_map/forward_tiles/pallas_call | solution.py:220
  80.9 0.0 copy-start.2
  80.9 0.0 copy-start.3
  80.9 2.1 collective-permute-start.7
  83.0 1.9 collective-permute-done.7
  84.8 0.1 add_convert_fusion.1
  85.0 19.0 %all_to_all.46.parts = bf16[8,256,128]{2,1,0:T(8,128)(2,1)S(1)} all-to-all(bf16[8,256,128]{2,1,0:T(8,128)(2,1)S(1)} %bitcast.67), channel_id=1, replica_groups={{0,2,4,6,8,10,12,14},{1,3,5,7,9,11,13,15},{16,18,20,22,24,26,28,30},{17..., dimensions={0} | all-to-all | bytes 1048576 | tf_op jit(solution)/shard_map/all_to_all | solution.py:43
  104.0 0.9 layer.1
  104.8 14.2 %all_to_all.47.mine = bf16[8,288,128]{2,1,0:T(8,128)(2,1)S(1)} all-to-all(bf16[8,288,128]{2,1,0:T(8,128)(2,1)S(1)} %get-tuple-element.12), channel_id=1, replica_groups={{0,2,4,6,8,10,12,14},{1,3,5,7,9,11,13,15},{16,18,20,22,24,26,28,30},{17..., dimensions={0} | all-to-all | bytes 1179648 | tf_op jit(solution)/shard_map/all_to_all | solution.py:43
  119.0 1.9 collective-permute-start.8
  120.9 1.9 collective-permute-done.8.other
  122.9 3.4 %backward_tiles.1 = (bf16[4096,128]{1,0:T(8,128)(2,1)S(1)}, bf16[4096,128]{1,0:T(8,128)(2,1)S(1)}) custom-call(s32[4]{0:T(128)S(1)} %pad_add_fusion.meta, s32[128]{0:T(128)S(1)} %bitcast.65, s32[128]{0:T(128)S(1)} %fusion.3.places, bf16[128,128,128]{2,1,0:T(8,128)(2,1)S(1)} %bitcast.53, bf16[8,288,128]{2,1,0:T(8,128)(2,1)S(1)} %all_to_all.47.mine, ...), custom_call_target="tpu_custom_call" | custom-call | flops 536870912 | bytes 7340032 | tf_op jit(solution)/shard_map/backward_tiles/pallas_call | solution.py:254
  126.3 7.8 %collective-permute-start.10 = (bf16[4096,128]{1,0:T(8,128)(2,1)S(1)}, bf16[4096,128]{1,0:T(8,128)(2,1)}, u32[]{:S(2)}, u32[]{:S(2)}) collective-permute-start(bf16[4096,128]{1,0:T(8,128)(2,1)S(1)} %get-tuple-element.14), channel_id=1, source_target_pairs={{0,256},{16,272},{32,288},{48,304},{64,320},{80,336},{96,352},{112... | collective-permute-start | bytes 3145736 | tf_op jit(solution)/shard_map/ppermute | solution.py:28
  134.1 1.9 collective-permute-start.9
  136.0 21.8 %collective-permute-done.9 = f32[32,128]{1,0:T(8,128)S(1)} collective-permute-done((f32[32,128]{1,0:T(8,128)S(1)}, f32[32,128]{1,0:T(8,128)S(1)}, u32[]{:S(2)}, u32[]{:S(2)}) %collective-permute-start.9) | collective-permute-done | bytes 16416 | tf_op jit(solution)/shard_map/ppermute | solution.py:28
  157.9 0.7 broadcast_in_dim.24
  158.6 3.4 %all-to-all-start.3 = ((f32[16,32,128]{2,1,0:T(8,128)}), f32[16,32,128]{2,1,0:T(8,128)S(1)}, u32[]{:S(2)}, u32[]{:S(2)}) async-start(f32[16,32,128]{2,1,0:T(8,128)} %broadcast_in_dim.24), calls=%async_computation.3 | async-start | bytes 524288 | tf_op jit(solution)/shard_map/all_to_all | solution.py:43
  162.1 1.5 add_convert_fusion
  163.6 3.2 %collective-permute-start.11 = (bf16[1024,128]{1,0:T(8,128)(2,1)S(1)}, bf16[1024,128]{1,0:T(8,128)(2,1)S(1)}, u32[]{:S(2)}, u32[]{:S(2)}) collective-permute-start(bf16[1024,128]{1,0:T(8,128)(2,1)S(1)} %get-tuple-element.20), channel_id=1, source_target_pairs={{0,16},{16,32},{32,48},{48,64},{64,80},{80,96},{96,112},{112,128},... | collective-permute-start | bytes 786440 | tf_op jit(solution)/shard_map/ppermute | solution.py:28
  166.9 2.6 %collective-permute-start.12 = (bf16[1024,128]{1,0:T(8,128)(2,1)S(1)}, bf16[1024,128]{1,0:T(8,128)(2,1)S(1)}, u32[]{:S(2)}, u32[]{:S(2)}) collective-permute-start(bf16[1024,128]{1,0:T(8,128)(2,1)S(1)} %get-tuple-element.21), channel_id=1, source_target_pairs={{0,240},{16,0},{32,16},{48,32},{64,48},{80,64},{96,80},{112,96},{1... | collective-permute-start | bytes 786440 | tf_op jit(solution)/shard_map/ppermute | solution.py:28
  169.5 4.8 %collective-permute-start.13 = (bf16[512,128]{1,0:T(8,128)(2,1)S(1)}, bf16[512,128]{1,0:T(8,128)(2,1)S(1)}, u32[]{:S(2)}, u32[]{:S(2)}) collective-permute-start(bf16[512,128]{1,0:T(8,128)(2,1)S(1)} %get-tuple-element.18), channel_id=1, source_target_pairs={{0,32},{16,48},{32,64},{48,80},{64,96},{80,112},{96,128},{112,144}... | collective-permute-start | bytes 393224 | tf_op jit(solution)/shard_map/ppermute | solution.py:28
  174.3 3.1 %collective-permute-start.14 = (bf16[512,128]{1,0:T(8,128)(2,1)S(1)}, bf16[512,128]{1,0:T(8,128)(2,1)S(1)}, u32[]{:S(2)}, u32[]{:S(2)}) collective-permute-start(bf16[512,128]{1,0:T(8,128)(2,1)S(1)} %get-tuple-element.19), channel_id=1, source_target_pairs={{0,224},{16,240},{32,0},{48,16},{64,32},{80,48},{96,64},{112,80},{... | collective-permute-start | bytes 393224 | tf_op jit(solution)/shard_map/ppermute | solution.py:28
  177.5 3.4 %all-to-all-done.3 = f32[16,32,128]{2,1,0:T(8,128)S(1)} async-done(((f32[16,32,128]{2,1,0:T(8,128)}), f32[16,32,128]{2,1,0:T(8,128)S(1)}, u32[]{:S(2)}, u32[]{:S(2)}) %all-to-all-start.3) | async-done | bytes 262176 | tf_op jit(solution)/shard_map/all_to_all | solution.py:43
  180.9 0.7 broadcast_in_dim.26
  181.5 3.6 %all-to-all-start.4 = ((f32[8,32,128]{2,1,0:T(8,128)}), f32[8,32,128]{2,1,0:T(8,128)S(1)}, u32[]{:S(2)}, u32[]{:S(2)}) async-start(f32[8,32,128]{2,1,0:T(8,128)} %broadcast_in_dim.26), calls=%async_computation.4 | async-start | bytes 262144 | tf_op jit(solution)/shard_map/all_to_all | solution.py:43
  185.2 3.4 %collective-permute-done.13 = bf16[512,128]{1,0:T(8,128)(2,1)S(1)} collective-permute-done((bf16[512,128]{1,0:T(8,128)(2,1)S(1)}, bf16[512,128]{1,0:T(8,128)(2,1)S(1)}, u32[]{:S(2)}, u32[]{:S(2)}) %collective-permute-start.13) | collective-permute-done | bytes 131104 | tf_op jit(solution)/shard_map/ppermute | solution.py:28
  188.6 0.8 add_convert_fusion.2
  189.4 3.8 %all-to-all-done.4 = f32[8,32,128]{2,1,0:T(8,128)S(1)} async-done(((f32[8,32,128]{2,1,0:T(8,128)}), f32[8,32,128]{2,1,0:T(8,128)S(1)}, u32[]{:S(2)}, u32[]{:S(2)}) %all-to-all-start.4) | async-done | bytes 131104 | tf_op jit(solution)/shard_map/all_to_all | solution.py:43
  193.2 7.7 %all-to-all-start.5 = ((bf16[4,256,128]{2,1,0:T(8,128)(2,1)}), bf16[4,256,128]{2,1,0:T(8,128)(2,1)S(1)}, u32[]{:S(2)}, u32[]{:S(2)}) async-start(bf16[4,256,128]{2,1,0:T(8,128)(2,1)} %bitcast.27), calls=%async_computation.5 | async-start | bytes 524288 | tf_op jit(solution)/shard_map/all_to_all | solution.py:43
  201.0 0.1 copy.13
  201.1 0.8 copy.15
  201.8 18.3 %all-to-all-done.5 = bf16[4,256,128]{2,1,0:T(8,128)(2,1)S(1)} async-done(((bf16[4,256,128]{2,1,0:T(8,128)(2,1)}), bf16[4,256,128]{2,1,0:T(8,128)(2,1)S(1)}, u32[]{:S(2)}, u32[]{:S(2)}) %all-to-all-start.5) | async-done | bytes 262176 | tf_op jit(solution)/shard_map/all_to_all | solution.py:43
  220.2 0.8 copy.14
  (28 shorter events, 0.3 us)
Async XLA Ops:
  0.6 60.5 %copy-start.4 = (s32[1,1,128]{2,1,0:T(1,128)S(1)}, s32[1,1,128]{2,1,0:T(1,128)}, u32[]{:S(2)}) copy-start(s32[1,1,128]{2,1,0:T(1,128)} %param.12) | copy-start | bytes 1540
  0.6 74.5 %copy-start.5 = (s32[1,1,128]{2,1,0:T(1,128)S(1)}, s32[1,1,128]{2,1,0:T(1,128)}, u32[]{:S(2)}) copy-start(s32[1,1,128]{2,1,0:T(1,128)} %param.11) | copy-start | bytes 1540
  36.8 13.8 %collective-permute-start.1 = (bf16[1024,128]{1,0:T(8,128)(2,1)S(1)}, bf16[1024,128]{1,0:T(8,128)(2,1)S(1)}, u32[]{:S(2)}, u32[]{:S(2)}) collective-permute-start(bf16[1024,128]{1,0:T(8,128)(2,1)S(1)} %bitcast.54), channel_id=1, source_target_pairs={{0,240},{16,0},{32,16},{48,32},{64,48},{80,64},{96,80},{112,96},{1... | collective-permute-start | bytes 786440 | tf_op jit(solution)/shard_map/ppermute | solution.py:28
  38.7 12.2 %collective-permute-start = (bf16[1024,128]{1,0:T(8,128)(2,1)S(1)}, bf16[1024,128]{1,0:T(8,128)(2,1)S(1)}, u32[]{:S(2)}, u32[]{:S(2)}) collective-permute-start(bf16[1024,128]{1,0:T(8,128)(2,1)S(1)} %bitcast.55), channel_id=1, source_target_pairs={{0,16},{16,32},{32,48},{48,64},{64,80},{80,96},{96,112},{112,128},... | collective-permute-start | bytes 786440 | tf_op jit(solution)/shard_map/ppermute | solution.py:28
  42.7 14.8 %collective-permute-start.2 = (bf16[512,128]{1,0:T(8,128)(2,1)S(1)}, bf16[512,128]{1,0:T(8,128)(2,1)S(1)}, u32[]{:S(2)}, u32[]{:S(2)}) collective-permute-start(bf16[512,128]{1,0:T(8,128)(2,1)S(1)} %bitcast.73), channel_id=1, source_target_pairs={{0,32},{16,48},{32,64},{48,80},{64,96},{80,112},{96,128},{112,144}... | collective-permute-start | bytes 393224 | tf_op jit(solution)/shard_map/ppermute | solution.py:28
  45.1 12.4 %collective-permute-start.3 = (bf16[512,128]{1,0:T(8,128)(2,1)S(1)}, bf16[512,128]{1,0:T(8,128)(2,1)S(1)}, u32[]{:S(2)}, u32[]{:S(2)}) collective-permute-start(bf16[512,128]{1,0:T(8,128)(2,1)S(1)} %bitcast.72), channel_id=1, source_target_pairs={{0,224},{16,240},{32,0},{48,16},{64,32},{80,48},{96,64},{112,80},{... | collective-permute-start | bytes 393224 | tf_op jit(solution)/shard_map/ppermute | solution.py:28
  51.0 24.2 %collective-permute-start.5 = (bf16[2048,128]{1,0:T(8,128)(2,1)S(1)}, bf16[2048,128]{1,0:T(8,128)(2,1)S(1)}, u32[]{:S(2)}, u32[]{:S(2)}) collective-permute-start(bf16[2048,128]{1,0:T(8,128)(2,1)S(1)} %pad_maximum_fusion), channel_id=1, source_target_pairs={{0,256},{16,272},{32,288},{48,304},{64,320},{80,336},{96,352},{112... | collective-permute-start | bytes 1572872 | tf_op jit(solution)/shard_map/ppermute | solution.py:28
  55.1 17.2 %collective-permute-start.4 = (bf16[1024,128]{1,0:T(8,128)(2,1)S(1)}, bf16[1024,128]{1,0:T(8,128)(2,1)S(1)}, u32[]{:S(2)}, u32[]{:S(2)}) collective-permute-start(bf16[1024,128]{1,0:T(8,128)(2,1)S(1)} %bitcast.56), channel_id=1, source_target_pairs={{0,256},{16,272},{32,288},{48,304},{64,320},{80,336},{96,352},{112... | collective-permute-start | bytes 786440 | tf_op jit(solution)/shard_map/ppermute | solution.py:28
  57.6 17.6 %collective-permute-start.6 = (bf16[1024,128]{1,0:T(8,128)(2,1)S(1)}, bf16[1024,128]{1,0:T(8,128)(2,1)S(1)}, u32[]{:S(2)}, u32[]{:S(2)}) collective-permute-start(bf16[1024,128]{1,0:T(8,128)(2,1)S(1)} %pad_maximum_fusion.1), channel_id=1, source_target_pairs={{0,256},{16,272},{32,288},{48,304},{64,320},{80,336},{96,352},{112... | collective-permute-start | bytes 786440 | tf_op jit(solution)/shard_map/ppermute | solution.py:28
  75.2 2.2 copy-start
  80.9 23.1 %copy-start.2 = (bf16[256,256]{1,0:T(8,128)(2,1)S(1)}, bf16[256,256]{1,0:T(8,128)(2,1)}, u32[]{:S(2)}) copy-start(bf16[256,256]{1,0:T(8,128)(2,1)} %cotangent.1) | copy-start | bytes 393220
  80.9 23.1 %copy-start.3 = (bf16[128,256]{1,0:T(8,128)(2,1)S(1)}, bf16[128,256]{1,0:T(8,128)(2,1)}, u32[]{:S(2)}) copy-start(bf16[128,256]{1,0:T(8,128)(2,1)} %weight.1) | copy-start | bytes 196612
  80.9 3.9 %collective-permute-start.7 = (bf16[2048,128]{1,0:T(8,128)(2,1)S(1)}, bf16[2048,128]{1,0:T(8,128)(2,1)S(1)}, u32[]{:S(2)}, u32[]{:S(2)}) collective-permute-start(bf16[2048,128]{1,0:T(8,128)(2,1)S(1)} %get-tuple-element.10), channel_id=1, source_target_pairs={{0,1},{1,0},{2,3},{3,2},{4,5},{5,4},{6,7},{7,6},{8,9},{9,8},{10,11... | collective-permute-start | bytes 1572872 | tf_op jit(solution)/shard_map/ppermute | solution.py:32
  84.8 38.0 %copy-start.1 = (bf16[1,1,128,128,128]{4,3,2,1,0:T(8,128)(2,1)S(1)}, bf16[1,1,128,128,128]{4,3,2,1,0:T(8,128)(2,1)}, u32[]{:S(2)}) copy-start(bf16[1,1,128,128,128]{4,3,2,1,0:T(8,128)(2,1)} %param.10) | copy-start | bytes 12582916
  119.0 3.9 %collective-permute-start.8 = (bf16[8,288,128]{2,1,0:T(8,128)(2,1)S(1)}, bf16[8,288,128]{2,1,0:T(8,128)(2,1)S(1)}, u32[]{:S(2)}, u32[]{:S(2)}) collective-permute-start(bf16[8,288,128]{2,1,0:T(8,128)(2,1)S(1)} %all_to_all.47.mine), channel_id=1, source_target_pairs={{0,1},{1,0},{2,3},{3,2},{4,5},{5,4},{6,7},{7,6},{8,9},{9,8},{10,11... | collective-permute-start | bytes 1769480 | tf_op jit(solution)/shard_map/ppermute | solution.py:32
  126.3 35.8 %collective-permute-start.10 = (bf16[4096,128]{1,0:T(8,128)(2,1)S(1)}, bf16[4096,128]{1,0:T(8,128)(2,1)}, u32[]{:S(2)}, u32[]{:S(2)}) collective-permute-start(bf16[4096,128]{1,0:T(8,128)(2,1)S(1)} %get-tuple-element.14), channel_id=1, source_target_pairs={{0,256},{16,272},{32,288},{48,304},{64,320},{80,336},{96,352},{112... | collective-permute-start | bytes 3145736 | tf_op jit(solution)/shard_map/ppermute | solution.py:28
  134.1 23.8 %collective-permute-start.9 = (f32[32,128]{1,0:T(8,128)S(1)}, f32[32,128]{1,0:T(8,128)S(1)}, u32[]{:S(2)}, u32[]{:S(2)}) collective-permute-start(f32[32,128]{1,0:T(8,128)S(1)} %add_bitcast_fusion), channel_id=1, source_target_pairs={{0,256},{16,272},{32,288},{48,304},{64,320},{80,336},{96,352},{112... | collective-permute-start | bytes 49160 | tf_op jit(solution)/shard_map/ppermute | solution.py:28
  158.6 22.2 %all-to-all-start.3 = ((f32[16,32,128]{2,1,0:T(8,128)}), f32[16,32,128]{2,1,0:T(8,128)S(1)}, u32[]{:S(2)}, u32[]{:S(2)}) async-start(f32[16,32,128]{2,1,0:T(8,128)} %broadcast_in_dim.24), calls=%async_computation.3 | async-start | bytes 524288 | tf_op jit(solution)/shard_map/all_to_all | solution.py:43
  163.6 25.0 %collective-permute-start.11 = (bf16[1024,128]{1,0:T(8,128)(2,1)S(1)}, bf16[1024,128]{1,0:T(8,128)(2,1)S(1)}, u32[]{:S(2)}, u32[]{:S(2)}) collective-permute-start(bf16[1024,128]{1,0:T(8,128)(2,1)S(1)} %get-tuple-element.20), channel_id=1, source_target_pairs={{0,16},{16,32},{32,48},{48,64},{64,80},{80,96},{96,112},{112,128},... | collective-permute-start | bytes 786440 | tf_op jit(solution)/shard_map/ppermute | solution.py:28
  166.9 21.7 %collective-permute-start.12 = (bf16[1024,128]{1,0:T(8,128)(2,1)S(1)}, bf16[1024,128]{1,0:T(8,128)(2,1)S(1)}, u32[]{:S(2)}, u32[]{:S(2)}) collective-permute-start(bf16[1024,128]{1,0:T(8,128)(2,1)S(1)} %get-tuple-element.21), channel_id=1, source_target_pairs={{0,240},{16,0},{32,16},{48,32},{64,48},{80,64},{96,80},{112,96},{1... | collective-permute-start | bytes 786440 | tf_op jit(solution)/shard_map/ppermute | solution.py:28
  169.5 19.1 %collective-permute-start.13 = (bf16[512,128]{1,0:T(8,128)(2,1)S(1)}, bf16[512,128]{1,0:T(8,128)(2,1)S(1)}, u32[]{:S(2)}, u32[]{:S(2)}) collective-permute-start(bf16[512,128]{1,0:T(8,128)(2,1)S(1)} %get-tuple-element.18), channel_id=1, source_target_pairs={{0,32},{16,48},{32,64},{48,80},{64,96},{80,112},{96,128},{112,144}... | collective-permute-start | bytes 393224 | tf_op jit(solution)/shard_map/ppermute | solution.py:28
  174.3 14.3 %collective-permute-start.14 = (bf16[512,128]{1,0:T(8,128)(2,1)S(1)}, bf16[512,128]{1,0:T(8,128)(2,1)S(1)}, u32[]{:S(2)}, u32[]{:S(2)}) collective-permute-start(bf16[512,128]{1,0:T(8,128)(2,1)S(1)} %get-tuple-element.19), channel_id=1, source_target_pairs={{0,224},{16,240},{32,0},{48,16},{64,32},{80,48},{96,64},{112,80},{... | collective-permute-start | bytes 393224 | tf_op jit(solution)/shard_map/ppermute | solution.py:28
  181.5 11.7 %all-to-all-start.4 = ((f32[8,32,128]{2,1,0:T(8,128)}), f32[8,32,128]{2,1,0:T(8,128)S(1)}, u32[]{:S(2)}, u32[]{:S(2)}) async-start(f32[8,32,128]{2,1,0:T(8,128)} %broadcast_in_dim.26), calls=%async_computation.4 | async-start | bytes 262144 | tf_op jit(solution)/shard_map/all_to_all | solution.py:43
  193.2 26.9 %all-to-all-start.5 = ((bf16[4,256,128]{2,1,0:T(8,128)(2,1)}), bf16[4,256,128]{2,1,0:T(8,128)(2,1)S(1)}, u32[]{:S(2)}, u32[]{:S(2)}) async-start(bf16[4,256,128]{2,1,0:T(8,128)(2,1)} %bitcast.27), calls=%async_computation.5 | async-start | bytes 524288 | tf_op jit(solution)/shard_map/all_to_all | solution.py:43

commit v2 on v1

--- a/solution.py
+++ b/solution.py
@@ -17,8 +17,7 @@
 N_Y, N_ZH, N_ZL = 2, 4, 4
 N_Z = N_ZH * N_ZL
 N_PAIR, N_CORE = 8, 2
-CHUNK = 16
-UNROLL = 4
+UNROLL = 16
 
 
 def shift(x, dy, dz):
@@ -28,6 +27,16 @@
     return lax.ppermute(x, "row", pairs)
 
 
+def two_along_z(x):
+    width = N_PAIR * N_CORE
+    pairs = []
+    for row in range(N_Y * N_Z):
+        for col in range(width):
+            z = (row % N_Z + (2 if col % N_CORE else -2)) % N_Z
+            pairs.append((row * width + col, (row // N_Z * N_Z + z) * width + col))
+    return lax.ppermute(x, ("row", "col"), pairs)
+
+
 def swap_cores(x):
     return lax.ppermute(x, "col", [(c, c ^ 1) for c in range(N_PAIR * N_CORE)])
 
@@ -35,6 +44,11 @@
 Z_GROUPS = [[y * N_Z + z for z in range(N_Z)] for y in range(N_Y)]
 ZH_GROUPS = [
     [y * N_Z + zh * N_ZL + zl for zh in range(N_ZH)] for y in range(N_Y) for zl in range(N_ZL)
+]
+Y_PAIR_GROUPS = [
+    [(y * N_Z + z) * N_PAIR * N_CORE + p * N_CORE + core for y in range(N_Y) for p in range(N_PAIR)]
+    for z in range(N_Z)
+    for core in range(N_CORE)
 ]
 PAIR_GROUPS = [[p * N_CORE + core for p in range(N_PAIR)] for core in range(N_CORE)]
 
@@ -54,34 +68,24 @@
     return total
 
 
-def start_tiles(values_hbm, values, sems):
-    for c in range(values.shape[0] // CHUNK):
-        s = pl.ds(c * CHUNK, CHUNK)
-        pltpu.make_async_copy(values_hbm.at[s], values.at[s], sems.at[c]).start()
-
-
-def each_tile(count, values_hbm, values, sems, step):
-    def chunk(c, _):
-        s = pl.ds(c * CHUNK, CHUNK)
-        pltpu.make_async_copy(values_hbm.at[s], values.at[s], sems.at[c]).wait()
-        left = jnp.clip(count - c * CHUNK, 0, CHUNK)
-
-        def body(i, _):
-            step(c * CHUNK + i * UNROLL)
-            return 0
-
-        lax.fori_loop(0, (left + UNROLL - 1) // UNROLL, body, 0)
+def load_kernel(values_hbm, values, sem):
+    move = pltpu.make_async_copy(values_hbm, values, sem)
+    move.start()
+    move.wait()
+
+
+def each_tile(count, step):
+    def body(i, _):
+        step(i * UNROLL)
         return 0
 
-    lax.fori_loop(0, values.shape[0] // CHUNK, chunk, 0)
-
-
-def forward_kernel(meta, rows, places, values_hbm, z0, z1, z2, z3, z4, o0, o12, o34, keep, send,
-                   values, block, total, value_sems, block_sems):
-    start_tiles(values_hbm, values, value_sems)
-    q = z0.shape[0]
-    moves = [(z0, 0), (z1, q), (z2, 2 * q), (z3, 3 * q), (z4, 3 * q + q // 2), (o0, 4 * q),
-             (o12, 5 * q), (o34, 7 * q)]
+    lax.fori_loop(0, (count + UNROLL - 1) // UNROLL, body, 0)
+
+
+def forward_kernel(meta, rows, places, values, both, z1, z2, z3, o3, keep, send,
+                   block, total, block_sems):
+    q = z3.shape[0]
+    moves = [(both, 0), (z1, 2 * q), (z2, 4 * q), (z3, 6 * q), (o3, 7 * q)]
     moves = [
         pltpu.make_async_copy(src, block.at[pl.ds(at, src.shape[0])], block_sems.at[i])
         for i, (src, at) in enumerate(moves)
@@ -104,7 +108,7 @@
             row = jnp.where(first + u < count, rows[first + u], dump)
             total[row] += products[u]
 
-    each_tile(count, values_hbm, values, value_sems, step)
+    each_tile(count, step)
     tile = total.shape[1]
     for p in range(N_PAIR):
         for i in range(2):
@@ -138,9 +142,8 @@
         payload[p, 2 * width:] = local[k:k + share, p // half * width:(p // half + 1) * width]
 
 
-def backward_kernel(meta, cols, places, values_hbm, mine, other, keep, send,
-                    values, block, total, value_sems, block_sems):
-    start_tiles(values_hbm, values, value_sems)
+def backward_kernel(meta, cols, places, values, mine, other, keep_far, keep_own, send_far, send_own,
+                    block, total, block_sems):
     pairs, two = block.shape[1], block.shape[2]
     moves = [
         pltpu.make_async_copy(src.at[:, pl.ds(0, two)], block.at[i], block_sems.at[i])
@@ -167,12 +170,18 @@
             col = jnp.where(first + u < count, cols[first + u], dump)
             total[col] += products[u]
 
-    each_tile(count, values_hbm, values, value_sems, step)
-    for d, offset in enumerate((0, 1, 3, 2)):
+    each_tile(count, step)
+    classes = (
+        (0, keep_own, send_own, 0),
+        (1, keep_far, send_far, 0),
+        (3, keep_far, send_far, 1),
+        (2, keep_far, send_far, 2),
+    )
+    for offset, keep, send, place in classes:
         zl = (my_zl + offset) % N_ZL
         for zh in range(N_ZH):
             for i in range(2):
-                at = pl.ds(((d * N_ZH + zh) * 2 + i) * tile, tile)
+                at = pl.ds(((place * N_ZH + zh) * 2 + i) * tile, tile)
                 keep[at] = total[(my_y * N_Z + zh * N_ZL + zl) * 2 + i].astype(BF16)
                 send[at] = total[((1 - my_y) * N_Z + zh * N_ZL + zl) * 2 + i].astype(BF16)
 
@@ -187,7 +196,16 @@
     r = lax.axis_index("row")
     c = lax.axis_index("col")
     my_y, my_zl, core = r // N_Z, r % N_ZL, c % N_CORE
-    values = tile_values[0, 0]
+    params = pltpu.CompilerParams(vmem_limit_bytes=VMEM_LIMIT)
+    values = pl.pallas_call(
+        load_kernel,
+        out_shape=jax.ShapeDtypeStruct(tile_values.shape[2:], BF16),
+        in_specs=[ANY],
+        out_specs=VMEM,
+        scratch_shapes=[pltpu.SemaphoreType.DMA],
+        compiler_params=params,
+        name="load_tiles",
+    )(tile_values[0, 0])
     rows = tile_rows[0, 0]
     cols = tile_cols[0, 0]
     meta = jnp.stack([tile_count[0, 0], core, my_y, my_zl]).astype(jnp.int32)
@@ -195,38 +213,32 @@
     at = cols // 2
     distance = jnp.array([0, 2, 3, 1], jnp.int32)[(at - my_zl) % N_ZL]
     col_places = (
-        (((at // N_Z) ^ my_y) * N_ZL + distance) * N_ZH + at // N_ZL % N_ZH
+        (distance * N_Y + ((at // N_Z) ^ my_y)) * N_ZH + at // N_ZL % N_ZH
     ) * 2 + cols % 2
     at = rows // 2
     row_places = (((at % N_CORE) ^ core) * N_PAIR + at // N_CORE) * 2 + rows % 2
 
-    z0 = exchange(copies(features[0, 0], N_ZH).reshape(N_ZH * sub, width), "row", ZH_GROUPS)
-    half = z0.shape[0] // 2
-    z1, z2 = shift(z0, 0, 1), shift(z0, 0, -1)
-    z3, z4 = shift(z0[:half], 0, 2), shift(z0[half:], 0, -2)
+    z0 = lax.all_gather(features[0, 0], "row", axis=0, tiled=True, axis_index_groups=ZH_GROUPS)
     o0 = shift(z0, 1, 0)
-    o12 = shift(jnp.concatenate([z1, z2]), 1, 0)
-    o34 = shift(jnp.concatenate([z3, z4]), 1, 0)
-    pieces = [
-        piece.reshape(-1, tile, width) for piece in (z0, z1, z2, z3, z4, o0, o12, o34)
-    ]
-    n_chunks = slots // CHUNK
+    z3 = two_along_z(z0)
+    both = jnp.concatenate([z0, o0])
+    z1, z2 = shift(both, 0, 1), shift(both, 0, -1)
+    o3 = shift(z3, 1, 0)
+    pieces = [piece.reshape(-1, tile, width) for piece in (both, z1, z2, z3, o3)]
     rows_n = n_col * sub // tile
     cols_n = n_row * sub // tile
     half_rows = jax.ShapeDtypeStruct((n_col * sub // 2, width), BF16)
-    half_cols = jax.ShapeDtypeStruct((n_row * sub // 2, width), BF16)
+    one = jax.ShapeDtypeStruct((N_ZH * sub, width), BF16)
+    three = jax.ShapeDtypeStruct((3 * N_ZH * sub, width), BF16)
     flops = 2 * slots * tile * tile * width
-    params = pltpu.CompilerParams(vmem_limit_bytes=VMEM_LIMIT)
     keep, send = pl.pallas_call(
         forward_kernel,
         out_shape=(half_rows, half_rows),
-        in_specs=[SMEM, SMEM, SMEM] + [ANY] * 9,
+        in_specs=[SMEM, SMEM, SMEM, VMEM] + [ANY] * len(pieces),
         out_specs=(VMEM, VMEM),
         scratch_shapes=[
-            pltpu.VMEM((slots, tile, tile), BF16),
             pltpu.VMEM((cols_n, tile, width), BF16),
             pltpu.VMEM((rows_n + 1, tile, width), F32),
-            pltpu.SemaphoreType.DMA((n_chunks,)),
             pltpu.SemaphoreType.DMA((len(pieces),)),
         ],
         compiler_params=params,
@@ -251,16 +263,14 @@
 
     mine = exchange(payload.reshape(-1, width), "col", PAIR_GROUPS).reshape(payload.shape)
     other = swap_cores(mine)
-    keep, send = pl.pallas_call(
+    keep_far, keep_own, send_far, send_own = pl.pallas_call(
         backward_kernel,
-        out_shape=(half_cols, half_cols),
-        in_specs=[SMEM, SMEM, SMEM] + [ANY] * 3,
-        out_specs=(VMEM, VMEM),
+        out_shape=(three, one) * 2,
+        in_specs=[SMEM, SMEM, SMEM, VMEM] + [ANY] * 2,
+        out_specs=(VMEM,) * 4,
         scratch_shapes=[
-            pltpu.VMEM((slots, tile, tile), BF16),
             pltpu.VMEM((N_CORE, N_PAIR, sub, width), BF16),
             pltpu.VMEM((cols_n + 1, tile, width), F32),
-            pltpu.SemaphoreType.DMA((n_chunks,)),
             pltpu.SemaphoreType.DMA((N_CORE,)),
         ],
         compiler_params=params,
@@ -271,20 +281,24 @@
     shared = add_up([mine[p, sub:] for p in range(N_PAIR)]) + add_up(
         [other[p, sub:] for p in range(N_PAIR)]
     )
-    shared = shared + shift(shared, 1, 0)
+    send_far, shared = lax.optimization_barrier((send_far, shared))
+    across_far, across_own = shift(send_far, 1, 0), shift(send_own, 1, 0)
     along_z = exchange(copies(shared, N_Z).reshape(-1, width), "row", Z_GROUPS)
+
+    held = (keep_far.astype(F32) + across_far.astype(F32)).astype(BF16)
     along_z = along_z.reshape(N_Z, share, width)
     shared = add_up([along_z[z] for z in range(N_Z)])
-    summed = exchange(copies(shared, N_PAIR).reshape(-1, width), "col", PAIR_GROUPS)
-    summed = summed.reshape(2, width, width).transpose(1, 0, 2).reshape(width, 2 * width)
+    q = N_ZH * sub
+    far = two_along_z(held[2 * q:])
+    near = shift(held[:q], 0, 1), shift(held[q:2 * q], 0, -1)
+    summed = exchange(
+        copies(shared, N_Y * N_PAIR).reshape(-1, width), ("row", "col"), Y_PAIR_GROUPS
+    ).reshape(N_Y, 2, width, width)
+    near, far, summed = lax.optimization_barrier((near, far, summed))
+    held = add_up([keep_own, across_own, near[0], near[1], far]).astype(BF16)
+    far = exchange(held, "row", ZH_GROUPS).reshape(N_ZH, 2, width, tile)
+    summed = (summed[0] + summed[1]).transpose(1, 0, 2).reshape(width, 2 * width)
     weight_grad = summed * (1.0 / math.sqrt(sub * n_row * n_col))
-
-    held = (keep.astype(F32) + shift(send, 1, 0).astype(F32)).astype(BF16)
-    q = held.shape[0] // N_ZL
-    near = shift(held[q:2 * q], 0, 1), shift(held[2 * q:3 * q], 0, -1)
-    far = shift(held[3 * q:3 * q + q // 2], 0, 2), shift(held[3 * q + q // 2:], 0, -2)
-    held = add_up([held[:q], near[0], near[1], jnp.concatenate(far)]).astype(BF16)
-    far = exchange(held, "row", ZH_GROUPS).reshape(N_ZH, 2, width, tile)
     feature_grad = add_up([far[zh] for zh in range(N_ZH)]).transpose(0, 2, 1)
     return activations, weight_grad, feature_grad.reshape(1, 1, sub, width)
 

time: 222 us -> 173 us (0.78)
  the two profiles are of different devices: /device:TPU:32 before, /device:TPU:2 now
where the time goes in v2:
time: 173 us; the launch traced here: 172 us
  blocking collectives  59.6 us (34%)
  starting transfers between devices  55.1 us (32%)
  waiting for transfers between devices  44.3 us (26%)
  local copies, waits for them, and re-layouts  5.68 us (3%)
  Pallas kernels  4.7 us (3%)
    all_to_all x2, blocking collectives, exchange(): return lax.all_to_all(x, axis, 0, 0, tiled=True, axis_index_groups=groups)  32.5 us
    all_gather x1, blocking collectives, on_device(): lax.all_gather(features[0, 0], 'row', axis=0, tiled=True, axis_index_grou...  27.1 us
    ppermute x8, starting transfers between devices, shift(): return lax.ppermute(x, 'row', pairs)  24.2 us
    all_to_all x3, waiting for transfers between devices, exchange(): return lax.all_to_all(x, axis, 0, 0, tiled=True, axis_index_groups=groups)  23.4 us
    all_to_all x3, starting transfers between devices, exchange(): return lax.all_to_all(x, axis, 0, 0, tiled=True, axis_index_groups=groups)  20.1 us
    ppermute x8, waiting for transfers between devices, shift(): return lax.ppermute(x, 'row', pairs)  13.8 us
    ppermute x2, starting transfers between devices, two_along_z(): return lax.ppermute(x, ('row', 'col'), pairs)  6.82 us
    ppermute x2, starting transfers between devices, swap_cores(): return lax.ppermute(x, 'col', [(c, c ^ 1) for c in range(N_PAIR * N_CORE)])  3.96 us
  transfers between devices with their start and end apart: 15, of which 10 were waited for; matrix products, arithmetic and copies ran while one was open for 2% of the time, Pallas kernels for 0%

profile of v2, /device:TPU:2, one launch (start us, length us, event | category | flops | bytes accessed | tf_op | source)
XLA Modules:
  0.0 172.4 jit_solution(6130500755049861336)
XLA Ops:
  0.6 27.1 %all-gather = bf16[1,1,1024,128]{3,2,1,0:T(8,128)(2,1)S(1)} all-gather(bf16[1,1,256,128]{3,2,1,0:T(8,128)(2,1)} %param.8), channel_id=2, replica_groups={{0,64,128,192},{16,80,144,208},{32,96,160,224},{48,112,176,240},{256,32..., dimensions={2}, use_global_device_ids=true | all-gather | bytes 327680 | tf_op jit(solution)/shard_map/all_gather | solution.py:221
  27.7 3.5 %collective-permute-start = (bf16[1024,128]{1,0:T(8,128)(2,1)S(1)}, bf16[1024,128]{1,0:T(8,128)(2,1)S(1)}, u32[]{:S(2)}, u32[]{:S(2)}) collective-permute-start(bf16[1024,128]{1,0:T(8,128)(2,1)S(1)} %bitcast.58), channel_id=1, source_target_pairs={{0,256},{16,272},{32,288},{48,304},{64,320},{80,336},{96,352},{112... | collective-permute-start | bytes 786440 | tf_op jit(solution)/shard_map/ppermute | solution.py:27
  31.2 3.4 %collective-permute-start.3 = (bf16[1024,128]{1,0:T(8,128)(2,1)S(1)}, bf16[1024,128]{1,0:T(8,128)(2,1)S(1)}, u32[]{:S(2)}, u32[]{:S(2)}) collective-permute-start(bf16[1024,128]{1,0:T(8,128)(2,1)S(1)} %bitcast.59), channel_id=1, source_target_pairs={{0,224},{1,33},{2,226},{3,35},{4,228},{5,37},{6,230},{7,39},{8,232... | collective-permute-start | bytes 786440 | tf_op jit(solution)/shard_map/ppermute | solution.py:37
  34.6 1.4 collective-permute-done
  36.0 4.0 %collective-permute-start.2 = (bf16[2048,128]{1,0:T(8,128)(2,1)S(1)}, bf16[2048,128]{1,0:T(8,128)(2,1)S(1)}, u32[]{:S(2)}, u32[]{:S(2)}) collective-permute-start(bf16[2048,128]{1,0:T(8,128)(2,1)S(1)} %pad_maximum_fusion), channel_id=1, source_target_pairs={{0,240},{16,0},{32,16},{48,32},{64,48},{80,64},{96,80},{112,96},{1... | collective-permute-start | bytes 1572872 | tf_op jit(solution)/shard_map/ppermute | solution.py:27
  40.0 1.9 %collective-permute-start.1 = (bf16[2048,128]{1,0:T(8,128)(2,1)S(1)}, bf16[2048,128]{1,0:T(8,128)(2,1)S(1)}, u32[]{:S(2)}, u32[]{:S(2)}) collective-permute-start(bf16[2048,128]{1,0:T(8,128)(2,1)S(1)} %pad_maximum_fusion), channel_id=1, source_target_pairs={{0,16},{16,32},{32,48},{48,64},{64,80},{80,96},{96,112},{112,128},... | collective-permute-start | bytes 1572872 | tf_op jit(solution)/shard_map/ppermute | solution.py:27
  42.6 3.3 %collective-permute-done.3 = bf16[1024,128]{1,0:T(8,128)(2,1)S(1)} collective-permute-done((bf16[1024,128]{1,0:T(8,128)(2,1)S(1)}, bf16[1024,128]{1,0:T(8,128)(2,1)S(1)}, u32[]{:S(2)}, u32[]{:S(2)}) %collective-permute-start.3) | collective-permute-done | bytes 262176 | tf_op jit(solution)/shard_map/ppermute | solution.py:37
  45.9 1.9 %collective-permute-start.4 = (bf16[1024,128]{1,0:T(8,128)(2,1)S(1)}, bf16[1024,128]{1,0:T(8,128)(2,1)S(1)}, u32[]{:S(2)}, u32[]{:S(2)}) collective-permute-start(bf16[1024,128]{1,0:T(8,128)(2,1)S(1)} %collective-permute-done.3), channel_id=1, source_target_pairs={{0,256},{16,272},{32,288},{48,304},{64,320},{80,336},{96,352},{112... | collective-permute-start | bytes 786440 | tf_op jit(solution)/shard_map/ppermute | solution.py:27
  47.9 0.1 pad_add_fusion.meta
  48.0 2.2 %copy-done = bf16[1,1,128,128,128]{4,3,2,1,0:T(8,128)(2,1)S(1)} copy-done((bf16[1,1,128,128,128]{4,3,2,1,0:T(8,128)(2,1)S(1)}, bf16[1,1,128,128,128]{4,3,2,1,0:T(8,128)(2,1)}, u32[]{:S(2)}) %copy-start) | copy-done | bytes 4194328
  50.1 0.3 load_tiles.1.values
  50.4 0.4 copy-done.3
  50.8 3.3 %collective-permute-done.4 = bf16[1024,128]{1,0:T(8,128)(2,1)S(1)} collective-permute-done((bf16[1024,128]{1,0:T(8,128)(2,1)S(1)}, bf16[1024,128]{1,0:T(8,128)(2,1)S(1)}, u32[]{:S(2)}, u32[]{:S(2)}) %collective-permute-start.4) | collective-permute-done | bytes 262176 | tf_op jit(solution)/shard_map/ppermute | solution.py:27
  54.2 0.0 collective-permute-done.2
  54.2 0.0 collective-permute-done.1
  54.2 1.6 forward_tiles.1
  55.8 0.0 copy-start.1
  55.8 0.0 copy-start.2
  55.8 2.1 %collective-permute-start.5 = (bf16[2048,128]{1,0:T(8,128)(2,1)S(1)}, bf16[2048,128]{1,0:T(8,128)(2,1)S(1)}, u32[]{:S(2)}, u32[]{:S(2)}) collective-permute-start(bf16[2048,128]{1,0:T(8,128)(2,1)S(1)} %get-tuple-element.18), channel_id=1, source_target_pairs={{0,1},{1,0},{2,3},{3,2},{4,5},{5,4},{6,7},{7,6},{8,9},{9,8},{10,11... | collective-permute-start | bytes 1572872 | tf_op jit(solution)/shard_map/ppermute | solution.py:41
  57.9 1.9 %collective-permute-done.5 = bf16[2048,128]{1,0:T(8,128)(2,1)S(1)} collective-permute-done((bf16[2048,128]{1,0:T(8,128)(2,1)S(1)}, bf16[2048,128]{1,0:T(8,128)(2,1)S(1)}, u32[]{:S(2)}, u32[]{:S(2)}) %collective-permute-start.5) | collective-permute-done | bytes 524320 | tf_op jit(solution)/shard_map/ppermute | solution.py:41
  59.8 0.1 add_convert_fusion.1
  59.9 18.4 %all_to_all.36.parts = bf16[8,256,128]{2,1,0:T(8,128)(2,1)S(1)} all-to-all(bf16[8,256,128]{2,1,0:T(8,128)(2,1)S(1)} %bitcast.56), channel_id=1, replica_groups={{0,2,4,6,8,10,12,14},{1,3,5,7,9,11,13,15},{16,18,20,22,24,26,28,30},{17..., dimensions={0} | all-to-all | bytes 1048576 | tf_op jit(solution)/shard_map/all_to_all | solution.py:57
  78.3 0.9 layer.1
  79.2 14.1 %all_to_all.37.mine = bf16[8,288,128]{2,1,0:T(8,128)(2,1)S(1)} all-to-all(bf16[8,288,128]{2,1,0:T(8,128)(2,1)S(1)} %get-tuple-element.20), channel_id=1, replica_groups={{0,2,4,6,8,10,12,14},{1,3,5,7,9,11,13,15},{16,18,20,22,24,26,28,30},{17..., dimensions={0} | all-to-all | bytes 1179648 | tf_op jit(solution)/shard_map/all_to_all | solution.py:57
  93.3 1.9 %collective-permute-start.6 = (bf16[8,288,128]{2,1,0:T(8,128)(2,1)S(1)}, bf16[8,288,128]{2,1,0:T(8,128)(2,1)S(1)}, u32[]{:S(2)}, u32[]{:S(2)}) collective-permute-start(bf16[8,288,128]{2,1,0:T(8,128)(2,1)S(1)} %all_to_all.37.mine), channel_id=1, source_target_pairs={{0,1},{1,0},{2,3},{3,2},{4,5},{5,4},{6,7},{7,6},{8,9},{9,8},{10,11... | collective-permute-start | bytes 1769480 | tf_op jit(solution)/shard_map/ppermute | solution.py:41
  95.2 1.9 %collective-permute-done.6.other = bf16[8,288,128]{2,1,0:T(8,128)(2,1)S(1)} collective-permute-done((bf16[8,288,128]{2,1,0:T(8,128)(2,1)S(1)}, bf16[8,288,128]{2,1,0:T(8,128)(2,1)S(1)}, u32[]{:S(2)}, u32[]{:S(2)}) %collective-permute-start.6) | collective-permute-done | bytes 589856 | tf_op jit(solution)/shard_map/ppermute | solution.py:41
  97.2 1.9 %backward_tiles.1 = (bf16[3072,128]{1,0:T(8,128)(2,1)S(1)}, bf16[1024,128]{1,0:T(8,128)(2,1)S(1)}, bf16[3072,128]{1,0:T(8,128)(2,1)S(1)}, bf16[1024,128]{1,0:T(8,128)(2,1)S(1)}) custom-call(s32[4]{0:T(128)S(1)} %pad_add_fusion.meta, s32[128]{0:T(128)S(1)} %bitcast.54, s32[128]{0:T(128)S(1)} %fusion.3.places, bf16[128,128,128]{2,1,0:T(8,128)(2,1)S(1)} %load_tiles.1.values, ...), custom_call_target="tpu_custom_call" | custom-call | flops 536870912 | bytes 7340032 | tf_op jit(solution)/shard_map/backward_tiles/pallas_call | solution.py:266
  99.1 2.0 %collective-permute-start.7 = (bf16[3072,128]{1,0:T(8,128)(2,1)S(1)}, bf16[3072,128]{1,0:T(8,128)(2,1)S(1)}, u32[]{:S(2)}, u32[]{:S(2)}) collective-permute-start(bf16[3072,128]{1,0:T(8,128)(2,1)S(1)} %get-tuple-element.23), channel_id=1, source_target_pairs={{0,256},{16,272},{32,288},{48,304},{64,320},{80,336},{96,352},{112... | collective-permute-start | bytes 2359304 | tf_op jit(solution)/shard_map/ppermute | solution.py:27
  101.1 0.7 broadcast_in_dim.6
  101.8 8.2 %all-to-all-start.2 = ((f32[16,32,128]{2,1,0:T(8,128)}), f32[16,32,128]{2,1,0:T(8,128)S(1)}, u32[]{:S(2)}, u32[]{:S(2)}) async-start(f32[16,32,128]{2,1,0:T(8,128)} %broadcast_in_dim.6), calls=%async_computation.2 | async-start | bytes 524288 | tf_op jit(solution)/shard_map/all_to_all | solution.py:57
  110.0 3.9 %collective-permute-start.11 = (bf16[1024,128]{1,0:T(8,128)(2,1)S(1)}, bf16[1024,128]{1,0:T(8,128)(2,1)S(1)}, u32[]{:S(2)}, u32[]{:S(2)}) collective-permute-start(bf16[1024,128]{1,0:T(8,128)(2,1)S(1)} %get-tuple-element.27), channel_id=1, source_target_pairs={{0,256},{16,272},{32,288},{48,304},{64,320},{80,336},{96,352},{112... | collective-permute-start | bytes 786440 | tf_op jit(solution)/shard_map/ppermute | solution.py:27
  114.0 7.4 %collective-permute-done.7 = bf16[3072,128]{1,0:T(8,128)(2,1)S(1)} collective-permute-done((bf16[3072,128]{1,0:T(8,128)(2,1)S(1)}, bf16[3072,128]{1,0:T(8,128)(2,1)S(1)}, u32[]{:S(2)}, u32[]{:S(2)}) %collective-permute-start.7) | collective-permute-done | bytes 786464 | tf_op jit(solution)/shard_map/ppermute | solution.py:27
  121.4 0.2 add_convert_fusion
  121.6 0.1 fusion.12
  121.7 3.4 %collective-permute-start.10 = (bf16[1024,128]{1,0:T(8,128)(2,1)S(1)}, bf16[1024,128]{1,0:T(8,128)(2,1)S(1)}, u32[]{:S(2)}, u32[]{:S(2)}) collective-permute-start(bf16[1024,128]{1,0:T(8,128)(2,1)S(1)} %get-tuple-element.34), channel_id=1, source_target_pairs={{0,224},{1,33},{2,226},{3,35},{4,228},{5,37},{6,230},{7,39},{8,232... | collective-permute-start | bytes 786440 | tf_op jit(solution)/shard_map/ppermute | solution.py:37
  125.1 5.1 %collective-permute-start.9 = (bf16[1024,128]{1,0:T(8,128)(2,1)S(1)}, bf16[1024,128]{1,0:T(8,128)(2,1)S(1)}, u32[]{:S(2)}, u32[]{:S(2)}) collective-permute-start(bf16[1024,128]{1,0:T(8,128)(2,1)S(1)} %get-tuple-element.35), channel_id=1, source_target_pairs={{0,240},{16,0},{32,16},{48,32},{64,48},{80,64},{96,80},{112,96},{1... | collective-permute-start | bytes 786440 | tf_op jit(solution)/shard_map/ppermute | solution.py:27
  130.2 1.9 %collective-permute-start.8 = (bf16[1024,128]{1,0:T(8,128)(2,1)S(1)}, bf16[1024,128]{1,0:T(8,128)(2,1)S(1)}, u32[]{:S(2)}, u32[]{:S(2)}) collective-permute-start(bf16[1024,128]{1,0:T(8,128)(2,1)S(1)} %get-tuple-element.36), channel_id=1, source_target_pairs={{0,16},{16,32},{32,48},{48,64},{64,80},{80,96},{96,112},{112,128},... | collective-permute-start | bytes 786440 | tf_op jit(solution)/shard_map/ppermute | solution.py:27
  132.1 0.7 broadcast_in_dim.8
  132.8 5.2 %all-to-all-start.3 = ((f32[16,32,128]{2,1,0:T(8,128)}), f32[16,32,128]{2,1,0:T(8,128)S(1)}, u32[]{:S(2)}, u32[]{:S(2)}) async-start(f32[16,32,128]{2,1,0:T(8,128)} %broadcast_in_dim.8), calls=%async_computation.3 | async-start | bytes 524288 | tf_op jit(solution)/shard_map/all_to_all | solution.py:57
  138.1 1.2 collective-permute-done.9
  139.2 0.5 collective-permute-done.8
  139.7 5.8 %all-to-all-done.3 = f32[16,32,128]{2,1,0:T(8,128)S(1)} async-done(((f32[16,32,128]{2,1,0:T(8,128)}), f32[16,32,128]{2,1,0:T(8,128)S(1)}, u32[]{:S(2)}, u32[]{:S(2)}) %all-to-all-start.3) | async-done | bytes 262176 | tf_op jit(solution)/shard_map/all_to_all | solution.py:57
  145.5 0.9 add_convert_fusion.2
  146.3 6.7 %all-to-all-start.4 = ((bf16[4,256,128]{2,1,0:T(8,128)(2,1)}), bf16[4,256,128]{2,1,0:T(8,128)(2,1)S(1)}, u32[]{:S(2)}, u32[]{:S(2)}) async-start(bf16[4,256,128]{2,1,0:T(8,128)(2,1)} %bitcast.22), calls=%async_computation.4 | async-start | bytes 524288 | tf_op jit(solution)/shard_map/all_to_all | solution.py:57
  153.1 0.1 copy.13
  153.2 0.8 copy.15
  154.0 17.6 %all-to-all-done.4 = bf16[4,256,128]{2,1,0:T(8,128)(2,1)S(1)} async-done(((bf16[4,256,128]{2,1,0:T(8,128)(2,1)}), bf16[4,256,128]{2,1,0:T(8,128)(2,1)S(1)}, u32[]{:S(2)}, u32[]{:S(2)}) %all-to-all-start.4) | async-done | bytes 262176 | tf_op jit(solution)/shard_map/all_to_all | solution.py:57
  171.6 0.8 copy.14
  (16 shorter events, 0.2 us)
Async XLA Ops:
  27.7 8.3 %collective-permute-start = (bf16[1024,128]{1,0:T(8,128)(2,1)S(1)}, bf16[1024,128]{1,0:T(8,128)(2,1)S(1)}, u32[]{:S(2)}, u32[]{:S(2)}) collective-permute-start(bf16[1024,128]{1,0:T(8,128)(2,1)S(1)} %bitcast.58), channel_id=1, source_target_pairs={{0,256},{16,272},{32,288},{48,304},{64,320},{80,336},{96,352},{112... | collective-permute-start | bytes 786440 | tf_op jit(solution)/shard_map/ppermute | solution.py:27
  31.2 14.7 %collective-permute-start.3 = (bf16[1024,128]{1,0:T(8,128)(2,1)S(1)}, bf16[1024,128]{1,0:T(8,128)(2,1)S(1)}, u32[]{:S(2)}, u32[]{:S(2)}) collective-permute-start(bf16[1024,128]{1,0:T(8,128)(2,1)S(1)} %bitcast.59), channel_id=1, source_target_pairs={{0,224},{1,33},{2,226},{3,35},{4,228},{5,37},{6,230},{7,39},{8,232... | collective-permute-start | bytes 786440 | tf_op jit(solution)/shard_map/ppermute | solution.py:37
  36.0 18.1 %collective-permute-start.2 = (bf16[2048,128]{1,0:T(8,128)(2,1)S(1)}, bf16[2048,128]{1,0:T(8,128)(2,1)S(1)}, u32[]{:S(2)}, u32[]{:S(2)}) collective-permute-start(bf16[2048,128]{1,0:T(8,128)(2,1)S(1)} %pad_maximum_fusion), channel_id=1, source_target_pairs={{0,240},{16,0},{32,16},{48,32},{64,48},{80,64},{96,80},{112,96},{1... | collective-permute-start | bytes 1572872 | tf_op jit(solution)/shard_map/ppermute | solution.py:27
  40.0 14.2 %collective-permute-start.1 = (bf16[2048,128]{1,0:T(8,128)(2,1)S(1)}, bf16[2048,128]{1,0:T(8,128)(2,1)S(1)}, u32[]{:S(2)}, u32[]{:S(2)}) collective-permute-start(bf16[2048,128]{1,0:T(8,128)(2,1)S(1)} %pad_maximum_fusion), channel_id=1, source_target_pairs={{0,16},{16,32},{32,48},{48,64},{64,80},{80,96},{96,112},{112,128},... | collective-permute-start | bytes 1572872 | tf_op jit(solution)/shard_map/ppermute | solution.py:27
  45.9 8.3 %collective-permute-start.4 = (bf16[1024,128]{1,0:T(8,128)(2,1)S(1)}, bf16[1024,128]{1,0:T(8,128)(2,1)S(1)}, u32[]{:S(2)}, u32[]{:S(2)}) collective-permute-start(bf16[1024,128]{1,0:T(8,128)(2,1)S(1)} %collective-permute-done.3), channel_id=1, source_target_pairs={{0,256},{16,272},{32,288},{48,304},{64,320},{80,336},{96,352},{112... | collective-permute-start | bytes 786440 | tf_op jit(solution)/shard_map/ppermute | solution.py:27
  48.0 2.2 %copy-start = (bf16[1,1,128,128,128]{4,3,2,1,0:T(8,128)(2,1)S(1)}, bf16[1,1,128,128,128]{4,3,2,1,0:T(8,128)(2,1)}, u32[]{:S(2)}) copy-start(bf16[1,1,128,128,128]{4,3,2,1,0:T(8,128)(2,1)} %param.10) | copy-start | bytes 12582916
  50.1 0.7 copy-start.3
  50.1 4.0 %copy-start.4 = (s32[1,1,128]{2,1,0:T(1,128)S(1)}, s32[1,1,128]{2,1,0:T(1,128)}, u32[]{:S(2)}) copy-start(s32[1,1,128]{2,1,0:T(1,128)} %param.11) | copy-start | bytes 1540
  55.8 22.5 %copy-start.1 = (bf16[256,256]{1,0:T(8,128)(2,1)S(1)}, bf16[256,256]{1,0:T(8,128)(2,1)}, u32[]{:S(2)}) copy-start(bf16[256,256]{1,0:T(8,128)(2,1)} %cotangent.1) | copy-start | bytes 393220
  55.8 22.5 %copy-start.2 = (bf16[128,256]{1,0:T(8,128)(2,1)S(1)}, bf16[128,256]{1,0:T(8,128)(2,1)}, u32[]{:S(2)}) copy-start(bf16[128,256]{1,0:T(8,128)(2,1)} %weight.1) | copy-start | bytes 196612
  55.8 3.9 %collective-permute-start.5 = (bf16[2048,128]{1,0:T(8,128)(2,1)S(1)}, bf16[2048,128]{1,0:T(8,128)(2,1)S(1)}, u32[]{:S(2)}, u32[]{:S(2)}) collective-permute-start(bf16[2048,128]{1,0:T(8,128)(2,1)S(1)} %get-tuple-element.18), channel_id=1, source_target_pairs={{0,1},{1,0},{2,3},{3,2},{4,5},{5,4},{6,7},{7,6},{8,9},{9,8},{10,11... | collective-permute-start | bytes 1572872 | tf_op jit(solution)/shard_map/ppermute | solution.py:41
  93.3 3.9 %collective-permute-start.6 = (bf16[8,288,128]{2,1,0:T(8,128)(2,1)S(1)}, bf16[8,288,128]{2,1,0:T(8,128)(2,1)S(1)}, u32[]{:S(2)}, u32[]{:S(2)}) collective-permute-start(bf16[8,288,128]{2,1,0:T(8,128)(2,1)S(1)} %all_to_all.37.mine), channel_id=1, source_target_pairs={{0,1},{1,0},{2,3},{3,2},{4,5},{5,4},{6,7},{7,6},{8,9},{9,8},{10,11... | collective-permute-start | bytes 1769480 | tf_op jit(solution)/shard_map/ppermute | solution.py:41
  99.1 22.3 %collective-permute-start.7 = (bf16[3072,128]{1,0:T(8,128)(2,1)S(1)}, bf16[3072,128]{1,0:T(8,128)(2,1)S(1)}, u32[]{:S(2)}, u32[]{:S(2)}) collective-permute-start(bf16[3072,128]{1,0:T(8,128)(2,1)S(1)} %get-tuple-element.23), channel_id=1, source_target_pairs={{0,256},{16,272},{32,288},{48,304},{64,320},{80,336},{96,352},{112... | collective-permute-start | bytes 2359304 | tf_op jit(solution)/shard_map/ppermute | solution.py:27
  101.8 30.3 %all-to-all-start.2 = ((f32[16,32,128]{2,1,0:T(8,128)}), f32[16,32,128]{2,1,0:T(8,128)S(1)}, u32[]{:S(2)}, u32[]{:S(2)}) async-start(f32[16,32,128]{2,1,0:T(8,128)} %broadcast_in_dim.6), calls=%async_computation.2 | async-start | bytes 524288 | tf_op jit(solution)/shard_map/all_to_all | solution.py:57
  110.0 35.4 %collective-permute-start.11 = (bf16[1024,128]{1,0:T(8,128)(2,1)S(1)}, bf16[1024,128]{1,0:T(8,128)(2,1)S(1)}, u32[]{:S(2)}, u32[]{:S(2)}) collective-permute-start(bf16[1024,128]{1,0:T(8,128)(2,1)S(1)} %get-tuple-element.27), channel_id=1, source_target_pairs={{0,256},{16,272},{32,288},{48,304},{64,320},{80,336},{96,352},{112... | collective-permute-start | bytes 786440 | tf_op jit(solution)/shard_map/ppermute | solution.py:27
  121.7 16.4 %collective-permute-start.10 = (bf16[1024,128]{1,0:T(8,128)(2,1)S(1)}, bf16[1024,128]{1,0:T(8,128)(2,1)S(1)}, u32[]{:S(2)}, u32[]{:S(2)}) collective-permute-start(bf16[1024,128]{1,0:T(8,128)(2,1)S(1)} %get-tuple-element.34), channel_id=1, source_target_pairs={{0,224},{1,33},{2,226},{3,35},{4,228},{5,37},{6,230},{7,39},{8,232... | collective-permute-start | bytes 786440 | tf_op jit(solution)/shard_map/ppermute | solution.py:37
  125.1 14.2 %collective-permute-start.9 = (bf16[1024,128]{1,0:T(8,128)(2,1)S(1)}, bf16[1024,128]{1,0:T(8,128)(2,1)S(1)}, u32[]{:S(2)}, u32[]{:S(2)}) collective-permute-start(bf16[1024,128]{1,0:T(8,128)(2,1)S(1)} %get-tuple-element.35), channel_id=1, source_target_pairs={{0,240},{16,0},{32,16},{48,32},{64,48},{80,64},{96,80},{112,96},{1... | collective-permute-start | bytes 786440 | tf_op jit(solution)/shard_map/ppermute | solution.py:27
  130.2 9.6 %collective-permute-start.8 = (bf16[1024,128]{1,0:T(8,128)(2,1)S(1)}, bf16[1024,128]{1,0:T(8,128)(2,1)S(1)}, u32[]{:S(2)}, u32[]{:S(2)}) collective-permute-start(bf16[1024,128]{1,0:T(8,128)(2,1)S(1)} %get-tuple-element.36), channel_id=1, source_target_pairs={{0,16},{16,32},{32,48},{48,64},{64,80},{80,96},{96,112},{112,128},... | collective-permute-start | bytes 786440 | tf_op jit(solution)/shard_map/ppermute | solution.py:27
  132.8 12.6 %all-to-all-start.3 = ((f32[16,32,128]{2,1,0:T(8,128)}), f32[16,32,128]{2,1,0:T(8,128)S(1)}, u32[]{:S(2)}, u32[]{:S(2)}) async-start(f32[16,32,128]{2,1,0:T(8,128)} %broadcast_in_dim.8), calls=%async_computation.3 | async-start | bytes 524288 | tf_op jit(solution)/shard_map/all_to_all | solution.py:57
  146.3 25.2 %all-to-all-start.4 = ((bf16[4,256,128]{2,1,0:T(8,128)(2,1)}), bf16[4,256,128]{2,1,0:T(8,128)(2,1)S(1)}, u32[]{:S(2)}, u32[]{:S(2)}) async-start(bf16[4,256,128]{2,1,0:T(8,128)(2,1)} %bitcast.22), calls=%async_computation.4 | async-start | bytes 524288 | tf_op jit(solution)/shard_map/all_to_all | solution.py:57

commit v3 on v2

--- a/solution.py
+++ b/solution.py
@@ -17,7 +17,7 @@
 N_Y, N_ZH, N_ZL = 2, 4, 4
 N_Z = N_ZH * N_ZL
 N_PAIR, N_CORE = 8, 2
-UNROLL = 16
+UNROLL = 32
 
 
 def shift(x, dy, dz):
@@ -283,7 +283,7 @@
     )
     send_far, shared = lax.optimization_barrier((send_far, shared))
     across_far, across_own = shift(send_far, 1, 0), shift(send_own, 1, 0)
-    along_z = exchange(copies(shared, N_Z).reshape(-1, width), "row", Z_GROUPS)
+    along_z = exchange(copies(shared.astype(BF16), N_Z).reshape(-1, width), "row", Z_GROUPS)
 
     held = (keep_far.astype(F32) + across_far.astype(F32)).astype(BF16)
     along_z = along_z.reshape(N_Z, share, width)
@@ -292,12 +292,12 @@
     far = two_along_z(held[2 * q:])
     near = shift(held[:q], 0, 1), shift(held[q:2 * q], 0, -1)
     summed = exchange(
-        copies(shared, N_Y * N_PAIR).reshape(-1, width), ("row", "col"), Y_PAIR_GROUPS
+        copies(shared.astype(BF16), N_Y * N_PAIR).reshape(-1, width), ("row", "col"), Y_PAIR_GROUPS
     ).reshape(N_Y, 2, width, width)
     near, far, summed = lax.optimization_barrier((near, far, summed))
     held = add_up([keep_own, across_own, near[0], near[1], far]).astype(BF16)
     far = exchange(held, "row", ZH_GROUPS).reshape(N_ZH, 2, width, tile)
-    summed = (summed[0] + summed[1]).transpose(1, 0, 2).reshape(width, 2 * width)
+    summed = add_up([summed[0], summed[1]]).transpose(1, 0, 2).reshape(width, 2 * width)
     weight_grad = summed * (1.0 / math.sqrt(sub * n_row * n_col))
     feature_grad = add_up([far[zh] for zh in range(N_ZH)]).transpose(0, 2, 1)
     return activations, weight_grad, feature_grad.reshape(1, 1, sub, width)

time: 173 us -> 171 us (0.988)
  the two profiles are of different devices: /device:TPU:2 before, /device:TPU:32 now
where the time goes in v3:
time: 171 us; the launch traced here: 170 us
  blocking collectives  70.7 us (41%)
  starting transfers between devices  51.7 us (30%)
  waiting for transfers between devices  34.4 us (20%)
  Pallas kernels  5.53 us (3%)
  local copies, waits for them, and re-layouts  4.91 us (3%)
    all_to_all x3, blocking collectives, exchange(): return lax.all_to_all(x, axis, 0, 0, tiled=True, axis_index_groups=groups)  44.5 us
    all_gather x1, blocking collectives, on_device(): lax.all_gather(features[0, 0], 'row', axis=0, tiled=True, axis_index_grou...  26.2 us
    ppermute x8, starting transfers between devices, shift(): return lax.ppermute(x, 'row', pairs)  22.5 us
    all_to_all x2, waiting for transfers between devices, exchange(): return lax.all_to_all(x, axis, 0, 0, tiled=True, axis_index_groups=groups)  16.9 us
    all_to_all x2, starting transfers between devices, exchange(): return lax.all_to_all(x, axis, 0, 0, tiled=True, axis_index_groups=groups)  15.2 us
    ppermute x8, waiting for transfers between devices, shift(): return lax.ppermute(x, 'row', pairs)  11 us
    ppermute x2, starting transfers between devices, two_along_z(): return lax.ppermute(x, ('row', 'col'), pairs)  10.1 us
    ppermute x2, starting transfers between devices, swap_cores(): return lax.ppermute(x, 'col', [(c, c ^ 1) for c in range(N_PAIR * N_CORE)])  3.96 us
  transfers between devices with their start and end apart: 14, of which 8 were waited for; matrix products, arithmetic and copies ran while one was open for 1% of the time, Pallas kernels for 0%

profile of v3, /device:TPU:32, one launch (start us, length us, event | category | flops | bytes accessed | tf_op | source)
XLA Modules:
  0.0 170.3 jit_solution(1121445280530632771)
XLA Ops:
  0.6 26.2 %all-gather = bf16[1,1,1024,128]{3,2,1,0:T(8,128)(2,1)S(1)} all-gather(bf16[1,1,256,128]{3,2,1,0:T(8,128)(2,1)} %param.8), channel_id=2, replica_groups={{0,64,128,192},{16,80,144,208},{32,96,160,224},{48,112,176,240},{256,32..., dimensions={2}, use_global_device_ids=true | all-gather | bytes 327680 | tf_op jit(solution)/shard_map/all_gather | solution.py:221
  26.8 3.5 %collective-permute-start = (bf16[1024,128]{1,0:T(8,128)(2,1)S(1)}, bf16[1024,128]{1,0:T(8,128)(2,1)S(1)}, u32[]{:S(2)}, u32[]{:S(2)}) collective-permute-start(bf16[1024,128]{1,0:T(8,128)(2,1)S(1)} %bitcast.57), channel_id=1, source_target_pairs={{0,256},{16,272},{32,288},{48,304},{64,320},{80,336},{96,352},{112... | collective-permute-start | bytes 786440 | tf_op jit(solution)/shard_map/ppermute | solution.py:27
  30.3 4.4 %collective-permute-start.3 = (bf16[1024,128]{1,0:T(8,128)(2,1)S(1)}, bf16[1024,128]{1,0:T(8,128)(2,1)S(1)}, u32[]{:S(2)}, u32[]{:S(2)}) collective-permute-start(bf16[1024,128]{1,0:T(8,128)(2,1)S(1)} %bitcast.58), channel_id=1, source_target_pairs={{0,224},{1,33},{2,226},{3,35},{4,228},{5,37},{6,230},{7,39},{8,232... | collective-permute-start | bytes 786440 | tf_op jit(solution)/shard_map/ppermute | solution.py:37
  34.7 0.3 collective-permute-done
  35.1 2.9 %collective-permute-start.2 = (bf16[2048,128]{1,0:T(8,128)(2,1)S(1)}, bf16[2048,128]{1,0:T(8,128)(2,1)S(1)}, u32[]{:S(2)}, u32[]{:S(2)}) collective-permute-start(bf16[2048,128]{1,0:T(8,128)(2,1)S(1)} %pad_maximum_fusion), channel_id=1, source_target_pairs={{0,240},{16,0},{32,16},{48,32},{64,48},{80,64},{96,80},{112,96},{1... | collective-permute-start | bytes 1572872 | tf_op jit(solution)/shard_map/ppermute | solution.py:27
  38.1 2.9 %collective-permute-start.1 = (bf16[2048,128]{1,0:T(8,128)(2,1)S(1)}, bf16[2048,128]{1,0:T(8,128)(2,1)S(1)}, u32[]{:S(2)}, u32[]{:S(2)}) collective-permute-start(bf16[2048,128]{1,0:T(8,128)(2,1)S(1)} %pad_maximum_fusion), channel_id=1, source_target_pairs={{0,16},{16,32},{32,48},{48,64},{64,80},{80,96},{96,112},{112,128},... | collective-permute-start | bytes 1572872 | tf_op jit(solution)/shard_map/ppermute | solution.py:27
  41.7 2.7 %collective-permute-done.3 = bf16[1024,128]{1,0:T(8,128)(2,1)S(1)} collective-permute-done((bf16[1024,128]{1,0:T(8,128)(2,1)S(1)}, bf16[1024,128]{1,0:T(8,128)(2,1)S(1)}, u32[]{:S(2)}, u32[]{:S(2)}) %collective-permute-start.3) | collective-permute-done | bytes 262176 | tf_op jit(solution)/shard_map/ppermute | solution.py:37
  44.4 2.1 %collective-permute-start.4 = (bf16[1024,128]{1,0:T(8,128)(2,1)S(1)}, bf16[1024,128]{1,0:T(8,128)(2,1)S(1)}, u32[]{:S(2)}, u32[]{:S(2)}) collective-permute-start(bf16[1024,128]{1,0:T(8,128)(2,1)S(1)} %collective-permute-done.3), channel_id=1, source_target_pairs={{0,256},{16,272},{32,288},{48,304},{64,320},{80,336},{96,352},{112... | collective-permute-start | bytes 786440 | tf_op jit(solution)/shard_map/ppermute | solution.py:27
  46.5 0.1 pad_add_fusion.meta
  46.6 2.2 %copy-done = bf16[1,1,128,128,128]{4,3,2,1,0:T(8,128)(2,1)S(1)} copy-done((bf16[1,1,128,128,128]{4,3,2,1,0:T(8,128)(2,1)S(1)}, bf16[1,1,128,128,128]{4,3,2,1,0:T(8,128)(2,1)}, u32[]{:S(2)}) %copy-start) | copy-done | bytes 4194328
  48.8 0.3 load_tiles.1.values
  49.1 0.4 copy-done.3
  49.5 3.2 %collective-permute-done.4 = bf16[1024,128]{1,0:T(8,128)(2,1)S(1)} collective-permute-done((bf16[1024,128]{1,0:T(8,128)(2,1)S(1)}, bf16[1024,128]{1,0:T(8,128)(2,1)S(1)}, u32[]{:S(2)}, u32[]{:S(2)}) %collective-permute-start.4) | collective-permute-done | bytes 262176 | tf_op jit(solution)/shard_map/ppermute | solution.py:27
  52.6 0.1 collective-permute-done.2
  52.7 0.0 collective-permute-done.1
  52.7 2.0 %forward_tiles.1 = (bf16[2048,128]{1,0:T(8,128)(2,1)S(1)}, bf16[2048,128]{1,0:T(8,128)(2,1)S(1)}) custom-call(s32[4]{0:T(128)S(1)} %pad_add_fusion.meta, s32[128]{0:T(128)S(1)} %bitcast.55, s32[128]{0:T(128)S(1)} %fusion.2.places, bf16[128,128,128]{2,1,0:T(8,128)(2,1)S(1)} %load_tiles.1.values, bf16[16,128,128]{2,1,0:T(8,128)(2,1)S(1)} %bitcast.49, ...), custom_call_target="tpu_custom_call" | custom-call | flops 536870912 | bytes 7340032 | tf_op jit(solution)/shard_map/forward_tiles/pallas_call | solution.py:234
  54.7 0.0 copy-start.1
  54.7 0.0 copy-start.2
  54.8 2.1 %collective-permute-start.5 = (bf16[2048,128]{1,0:T(8,128)(2,1)S(1)}, bf16[2048,128]{1,0:T(8,128)(2,1)S(1)}, u32[]{:S(2)}, u32[]{:S(2)}) collective-permute-start(bf16[2048,128]{1,0:T(8,128)(2,1)S(1)} %get-tuple-element.18), channel_id=1, source_target_pairs={{0,1},{1,0},{2,3},{3,2},{4,5},{5,4},{6,7},{7,6},{8,9},{9,8},{10,11... | collective-permute-start | bytes 1572872 | tf_op jit(solution)/shard_map/ppermute | solution.py:41
  56.8 1.9 %collective-permute-done.5 = bf16[2048,128]{1,0:T(8,128)(2,1)S(1)} collective-permute-done((bf16[2048,128]{1,0:T(8,128)(2,1)S(1)}, bf16[2048,128]{1,0:T(8,128)(2,1)S(1)}, u32[]{:S(2)}, u32[]{:S(2)}) %collective-permute-start.5) | collective-permute-done | bytes 524320 | tf_op jit(solution)/shard_map/ppermute | solution.py:41
  58.7 0.1 add_convert_fusion.1
  58.8 18.6 %all_to_all.36.parts = bf16[8,256,128]{2,1,0:T(8,128)(2,1)S(1)} all-to-all(bf16[8,256,128]{2,1,0:T(8,128)(2,1)S(1)} %bitcast.56), channel_id=1, replica_groups={{0,2,4,6,8,10,12,14},{1,3,5,7,9,11,13,15},{16,18,20,22,24,26,28,30},{17..., dimensions={0} | all-to-all | bytes 1048576 | tf_op jit(solution)/shard_map/all_to_all | solution.py:57
  77.5 0.9 layer.1
  78.3 14.2 %all_to_all.37.mine = bf16[8,288,128]{2,1,0:T(8,128)(2,1)S(1)} all-to-all(bf16[8,288,128]{2,1,0:T(8,128)(2,1)S(1)} %get-tuple-element.20), channel_id=1, replica_groups={{0,2,4,6,8,10,12,14},{1,3,5,7,9,11,13,15},{16,18,20,22,24,26,28,30},{17..., dimensions={0} | all-to-all | bytes 1179648 | tf_op jit(solution)/shard_map/all_to_all | solution.py:57
  92.5 1.9 %collective-permute-start.6 = (bf16[8,288,128]{2,1,0:T(8,128)(2,1)S(1)}, bf16[8,288,128]{2,1,0:T(8,128)(2,1)S(1)}, u32[]{:S(2)}, u32[]{:S(2)}) collective-permute-start(bf16[8,288,128]{2,1,0:T(8,128)(2,1)S(1)} %all_to_all.37.mine), channel_id=1, source_target_pairs={{0,1},{1,0},{2,3},{3,2},{4,5},{5,4},{6,7},{7,6},{8,9},{9,8},{10,11... | collective-permute-start | bytes 1769480 | tf_op jit(solution)/shard_map/ppermute | solution.py:41
  94.4 1.9 %collective-permute-done.6.other = bf16[8,288,128]{2,1,0:T(8,128)(2,1)S(1)} collective-permute-done((bf16[8,288,128]{2,1,0:T(8,128)(2,1)S(1)}, bf16[8,288,128]{2,1,0:T(8,128)(2,1)S(1)}, u32[]{:S(2)}, u32[]{:S(2)}) %collective-permute-start.6) | collective-permute-done | bytes 589856 | tf_op jit(solution)/shard_map/ppermute | solution.py:41
  96.4 2.4 %backward_tiles.1 = (bf16[3072,128]{1,0:T(8,128)(2,1)S(1)}, bf16[1024,128]{1,0:T(8,128)(2,1)S(1)}, bf16[3072,128]{1,0:T(8,128)(2,1)S(1)}, bf16[1024,128]{1,0:T(8,128)(2,1)S(1)}) custom-call(s32[4]{0:T(128)S(1)} %pad_add_fusion.meta, s32[128]{0:T(128)S(1)} %bitcast.54, s32[128]{0:T(128)S(1)} %fusion.3.places, bf16[128,128,128]{2,1,0:T(8,128)(2,1)S(1)} %load_tiles.1.values, ...), custom_call_target="tpu_custom_call" | custom-call | flops 536870912 | bytes 7340032 | tf_op jit(solution)/shard_map/backward_tiles/pallas_call | solution.py:266
  98.8 1.9 %collective-permute-start.7 = (bf16[3072,128]{1,0:T(8,128)(2,1)S(1)}, bf16[3072,128]{1,0:T(8,128)(2,1)S(1)}, u32[]{:S(2)}, u32[]{:S(2)}) collective-permute-start(bf16[3072,128]{1,0:T(8,128)(2,1)S(1)} %get-tuple-element.23), channel_id=1, source_target_pairs={{0,256},{16,272},{32,288},{48,304},{64,320},{80,336},{96,352},{112... | collective-permute-start | bytes 2359304 | tf_op jit(solution)/shard_map/ppermute | solution.py:27
  100.7 0.7 broadcast_in_dim.6
  101.4 9.0 %all-to-all-start.2 = ((bf16[16,32,128]{2,1,0:T(8,128)(2,1)}), bf16[16,32,128]{2,1,0:T(8,128)(2,1)S(1)}, u32[]{:S(2)}, u32[]{:S(2)}) async-start(bf16[16,32,128]{2,1,0:T(8,128)(2,1)} %broadcast_in_dim.6), calls=%async_computation.2 | async-start | bytes 262144 | tf_op jit(solution)/shard_map/all_to_all | solution.py:57
  110.4 3.3 %collective-permute-start.11 = (bf16[1024,128]{1,0:T(8,128)(2,1)S(1)}, bf16[1024,128]{1,0:T(8,128)(2,1)S(1)}, u32[]{:S(2)}, u32[]{:S(2)}) collective-permute-start(bf16[1024,128]{1,0:T(8,128)(2,1)S(1)} %get-tuple-element.27), channel_id=1, source_target_pairs={{0,256},{16,272},{32,288},{48,304},{64,320},{80,336},{96,352},{112... | collective-permute-start | bytes 786440 | tf_op jit(solution)/shard_map/ppermute | solution.py:27
  113.8 7.4 %collective-permute-done.7 = bf16[3072,128]{1,0:T(8,128)(2,1)S(1)} collective-permute-done((bf16[3072,128]{1,0:T(8,128)(2,1)S(1)}, bf16[3072,128]{1,0:T(8,128)(2,1)S(1)}, u32[]{:S(2)}, u32[]{:S(2)}) %collective-permute-start.7) | collective-permute-done | bytes 786464 | tf_op jit(solution)/shard_map/ppermute | solution.py:27
  121.2 0.2 add_convert_fusion
  121.4 0.1 fusion.12
  121.4 5.7 %collective-permute-start.10 = (bf16[1024,128]{1,0:T(8,128)(2,1)S(1)}, bf16[1024,128]{1,0:T(8,128)(2,1)S(1)}, u32[]{:S(2)}, u32[]{:S(2)}) collective-permute-start(bf16[1024,128]{1,0:T(8,128)(2,1)S(1)} %get-tuple-element.34), channel_id=1, source_target_pairs={{0,224},{1,33},{2,226},{3,35},{4,228},{5,37},{6,230},{7,39},{8,232... | collective-permute-start | bytes 786440 | tf_op jit(solution)/shard_map/ppermute | solution.py:37
  127.1 1.9 %collective-permute-start.9 = (bf16[1024,128]{1,0:T(8,128)(2,1)S(1)}, bf16[1024,128]{1,0:T(8,128)(2,1)S(1)}, u32[]{:S(2)}, u32[]{:S(2)}) collective-permute-start(bf16[1024,128]{1,0:T(8,128)(2,1)S(1)} %get-tuple-element.35), channel_id=1, source_target_pairs={{0,240},{16,0},{32,16},{48,32},{64,48},{80,64},{96,80},{112,96},{1... | collective-permute-start | bytes 786440 | tf_op jit(solution)/shard_map/ppermute | solution.py:27
  129.0 3.9 %collective-permute-start.8 = (bf16[1024,128]{1,0:T(8,128)(2,1)S(1)}, bf16[1024,128]{1,0:T(8,128)(2,1)S(1)}, u32[]{:S(2)}, u32[]{:S(2)}) collective-permute-start(bf16[1024,128]{1,0:T(8,128)(2,1)S(1)} %get-tuple-element.36), channel_id=1, source_target_pairs={{0,16},{16,32},{32,48},{48,64},{64,80},{80,96},{96,112},{112,128},... | collective-permute-start | bytes 786440 | tf_op jit(solution)/shard_map/ppermute | solution.py:27
  132.9 0.0 all-to-all-done.2
  133.0 11.7 %all_to_all.38 = bf16[16,32,128]{2,1,0:T(8,128)(2,1)S(1)} all-to-all(bf16[16,32,128]{2,1,0:T(8,128)(2,1)S(1)} %broadcast_in_dim.8), channel_id=1, replica_groups={{0,2,4,6,8,10,12,14,256,258,260,262,264,266,268,270},{1,3,5,7,9,11,13,1..., dimensions={0} | all-to-all | bytes 262144 | tf_op jit(solution)/shard_map/all_to_all | solution.py:57
  144.7 0.0 collective-permute-done.10
  144.7 0.0 collective-permute-done.9
  144.7 0.0 collective-permute-done.8
  144.8 0.9 add_convert_fusion.2
  145.6 6.1 %all-to-all-start.4 = ((bf16[4,256,128]{2,1,0:T(8,128)(2,1)}), bf16[4,256,128]{2,1,0:T(8,128)(2,1)S(1)}, u32[]{:S(2)}, u32[]{:S(2)}) async-start(bf16[4,256,128]{2,1,0:T(8,128)(2,1)} %bitcast.22), calls=%async_computation.4 | async-start | bytes 524288 | tf_op jit(solution)/shard_map/all_to_all | solution.py:57
  151.8 0.1 copy.13
  151.9 0.8 copy.15
  152.7 16.9 %all-to-all-done.4 = bf16[4,256,128]{2,1,0:T(8,128)(2,1)S(1)} async-done(((bf16[4,256,128]{2,1,0:T(8,128)(2,1)}), bf16[4,256,128]{2,1,0:T(8,128)(2,1)S(1)}, u32[]{:S(2)}, u32[]{:S(2)}) %all-to-all-start.4) | async-done | bytes 262176 | tf_op jit(solution)/shard_map/all_to_all | solution.py:57
  169.6 0.8 copy.14
  (15 shorter events, 0.2 us)
Async XLA Ops:
  26.8 8.3 %collective-permute-start = (bf16[1024,128]{1,0:T(8,128)(2,1)S(1)}, bf16[1024,128]{1,0:T(8,128)(2,1)S(1)}, u32[]{:S(2)}, u32[]{:S(2)}) collective-permute-start(bf16[1024,128]{1,0:T(8,128)(2,1)S(1)} %bitcast.57), channel_id=1, source_target_pairs={{0,256},{16,272},{32,288},{48,304},{64,320},{80,336},{96,352},{112... | collective-permute-start | bytes 786440 | tf_op jit(solution)/shard_map/ppermute | solution.py:27
  30.3 14.1 %collective-permute-start.3 = (bf16[1024,128]{1,0:T(8,128)(2,1)S(1)}, bf16[1024,128]{1,0:T(8,128)(2,1)S(1)}, u32[]{:S(2)}, u32[]{:S(2)}) collective-permute-start(bf16[1024,128]{1,0:T(8,128)(2,1)S(1)} %bitcast.58), channel_id=1, source_target_pairs={{0,224},{1,33},{2,226},{3,35},{4,228},{5,37},{6,230},{7,39},{8,232... | collective-permute-start | bytes 786440 | tf_op jit(solution)/shard_map/ppermute | solution.py:37
  35.1 17.6 %collective-permute-start.2 = (bf16[2048,128]{1,0:T(8,128)(2,1)S(1)}, bf16[2048,128]{1,0:T(8,128)(2,1)S(1)}, u32[]{:S(2)}, u32[]{:S(2)}) collective-permute-start(bf16[2048,128]{1,0:T(8,128)(2,1)S(1)} %pad_maximum_fusion), channel_id=1, source_target_pairs={{0,240},{16,0},{32,16},{48,32},{64,48},{80,64},{96,80},{112,96},{1... | collective-permute-start | bytes 1572872 | tf_op jit(solution)/shard_map/ppermute | solution.py:27
  38.1 14.7 %collective-permute-start.1 = (bf16[2048,128]{1,0:T(8,128)(2,1)S(1)}, bf16[2048,128]{1,0:T(8,128)(2,1)S(1)}, u32[]{:S(2)}, u32[]{:S(2)}) collective-permute-start(bf16[2048,128]{1,0:T(8,128)(2,1)S(1)} %pad_maximum_fusion), channel_id=1, source_target_pairs={{0,16},{16,32},{32,48},{48,64},{64,80},{80,96},{96,112},{112,128},... | collective-permute-start | bytes 1572872 | tf_op jit(solution)/shard_map/ppermute | solution.py:27
  44.4 8.3 %collective-permute-start.4 = (bf16[1024,128]{1,0:T(8,128)(2,1)S(1)}, bf16[1024,128]{1,0:T(8,128)(2,1)S(1)}, u32[]{:S(2)}, u32[]{:S(2)}) collective-permute-start(bf16[1024,128]{1,0:T(8,128)(2,1)S(1)} %collective-permute-done.3), channel_id=1, source_target_pairs={{0,256},{16,272},{32,288},{48,304},{64,320},{80,336},{96,352},{112... | collective-permute-start | bytes 786440 | tf_op jit(solution)/shard_map/ppermute | solution.py:27
  46.6 2.2 %copy-start = (bf16[1,1,128,128,128]{4,3,2,1,0:T(8,128)(2,1)S(1)}, bf16[1,1,128,128,128]{4,3,2,1,0:T(8,128)(2,1)}, u32[]{:S(2)}) copy-start(bf16[1,1,128,128,128]{4,3,2,1,0:T(8,128)(2,1)} %param.10) | copy-start | bytes 12582916
  48.8 0.7 copy-start.3
  48.8 3.9 %copy-start.4 = (s32[1,1,128]{2,1,0:T(1,128)S(1)}, s32[1,1,128]{2,1,0:T(1,128)}, u32[]{:S(2)}) copy-start(s32[1,1,128]{2,1,0:T(1,128)} %param.11) | copy-start | bytes 1540
  54.7 22.7 %copy-start.1 = (bf16[256,256]{1,0:T(8,128)(2,1)S(1)}, bf16[256,256]{1,0:T(8,128)(2,1)}, u32[]{:S(2)}) copy-start(bf16[256,256]{1,0:T(8,128)(2,1)} %cotangent.1) | copy-start | bytes 393220
  54.7 22.7 %copy-start.2 = (bf16[128,256]{1,0:T(8,128)(2,1)S(1)}, bf16[128,256]{1,0:T(8,128)(2,1)}, u32[]{:S(2)}) copy-start(bf16[128,256]{1,0:T(8,128)(2,1)} %weight.1) | copy-start | bytes 196612
  54.8 3.9 %collective-permute-start.5 = (bf16[2048,128]{1,0:T(8,128)(2,1)S(1)}, bf16[2048,128]{1,0:T(8,128)(2,1)S(1)}, u32[]{:S(2)}, u32[]{:S(2)}) collective-permute-start(bf16[2048,128]{1,0:T(8,128)(2,1)S(1)} %get-tuple-element.18), channel_id=1, source_target_pairs={{0,1},{1,0},{2,3},{3,2},{4,5},{5,4},{6,7},{7,6},{8,9},{9,8},{10,11... | collective-permute-start | bytes 1572872 | tf_op jit(solution)/shard_map/ppermute | solution.py:41
  92.5 3.9 %collective-permute-start.6 = (bf16[8,288,128]{2,1,0:T(8,128)(2,1)S(1)}, bf16[8,288,128]{2,1,0:T(8,128)(2,1)S(1)}, u32[]{:S(2)}, u32[]{:S(2)}) collective-permute-start(bf16[8,288,128]{2,1,0:T(8,128)(2,1)S(1)} %all_to_all.37.mine), channel_id=1, source_target_pairs={{0,1},{1,0},{2,3},{3,2},{4,5},{5,4},{6,7},{7,6},{8,9},{9,8},{10,11... | collective-permute-start | bytes 1769480 | tf_op jit(solution)/shard_map/ppermute | solution.py:41
  98.8 22.4 %collective-permute-start.7 = (bf16[3072,128]{1,0:T(8,128)(2,1)S(1)}, bf16[3072,128]{1,0:T(8,128)(2,1)S(1)}, u32[]{:S(2)}, u32[]{:S(2)}) collective-permute-start(bf16[3072,128]{1,0:T(8,128)(2,1)S(1)} %get-tuple-element.23), channel_id=1, source_target_pairs={{0,256},{16,272},{32,288},{48,304},{64,320},{80,336},{96,352},{112... | collective-permute-start | bytes 2359304 | tf_op jit(solution)/shard_map/ppermute | solution.py:27
  101.4 31.6 %all-to-all-start.2 = ((bf16[16,32,128]{2,1,0:T(8,128)(2,1)}), bf16[16,32,128]{2,1,0:T(8,128)(2,1)S(1)}, u32[]{:S(2)}, u32[]{:S(2)}) async-start(bf16[16,32,128]{2,1,0:T(8,128)(2,1)} %broadcast_in_dim.6), calls=%async_computation.2 | async-start | bytes 262144 | tf_op jit(solution)/shard_map/all_to_all | solution.py:57
  110.4 34.3 %collective-permute-start.11 = (bf16[1024,128]{1,0:T(8,128)(2,1)S(1)}, bf16[1024,128]{1,0:T(8,128)(2,1)S(1)}, u32[]{:S(2)}, u32[]{:S(2)}) collective-permute-start(bf16[1024,128]{1,0:T(8,128)(2,1)S(1)} %get-tuple-element.27), channel_id=1, source_target_pairs={{0,256},{16,272},{32,288},{48,304},{64,320},{80,336},{96,352},{112... | collective-permute-start | bytes 786440 | tf_op jit(solution)/shard_map/ppermute | solution.py:27
  121.4 23.3 %collective-permute-start.10 = (bf16[1024,128]{1,0:T(8,128)(2,1)S(1)}, bf16[1024,128]{1,0:T(8,128)(2,1)S(1)}, u32[]{:S(2)}, u32[]{:S(2)}) collective-permute-start(bf16[1024,128]{1,0:T(8,128)(2,1)S(1)} %get-tuple-element.34), channel_id=1, source_target_pairs={{0,224},{1,33},{2,226},{3,35},{4,228},{5,37},{6,230},{7,39},{8,232... | collective-permute-start | bytes 786440 | tf_op jit(solution)/shard_map/ppermute | solution.py:37
  127.1 17.6 %collective-permute-start.9 = (bf16[1024,128]{1,0:T(8,128)(2,1)S(1)}, bf16[1024,128]{1,0:T(8,128)(2,1)S(1)}, u32[]{:S(2)}, u32[]{:S(2)}) collective-permute-start(bf16[1024,128]{1,0:T(8,128)(2,1)S(1)} %get-tuple-element.35), channel_id=1, source_target_pairs={{0,240},{16,0},{32,16},{48,32},{64,48},{80,64},{96,80},{112,96},{1... | collective-permute-start | bytes 786440 | tf_op jit(solution)/shard_map/ppermute | solution.py:27
  129.0 15.7 %collective-permute-start.8 = (bf16[1024,128]{1,0:T(8,128)(2,1)S(1)}, bf16[1024,128]{1,0:T(8,128)(2,1)S(1)}, u32[]{:S(2)}, u32[]{:S(2)}) collective-permute-start(bf16[1024,128]{1,0:T(8,128)(2,1)S(1)} %get-tuple-element.36), channel_id=1, source_target_pairs={{0,16},{16,32},{32,48},{48,64},{64,80},{80,96},{96,112},{112,128},... | collective-permute-start | bytes 786440 | tf_op jit(solution)/shard_map/ppermute | solution.py:27
  145.6 23.9 %all-to-all-start.4 = ((bf16[4,256,128]{2,1,0:T(8,128)(2,1)}), bf16[4,256,128]{2,1,0:T(8,128)(2,1)S(1)}, u32[]{:S(2)}, u32[]{:S(2)}) async-start(bf16[4,256,128]{2,1,0:T(8,128)(2,1)} %bitcast.22), calls=%async_computation.4 | async-start | bytes 524288 | tf_op jit(solution)/shard_map/all_to_all | solution.py:57

commit v4 on v3

--- a/solution.py
+++ b/solution.py
@@ -18,6 +18,13 @@
 N_Z = N_ZH * N_ZL
 N_PAIR, N_CORE = 8, 2
 UNROLL = 32
+PREPARE = 8
+
+SLOT_BITS, ROW_BITS, BLOCK_BITS, COL_BITS, OWN_BIT = (0, 7), (7, 4), (11, 6), (17, 6), 23
+
+
+def field(entry, bits):
+    return (entry >> bits[0]) & ((1 << bits[1]) - 1)
 
 
 def shift(x, dy, dz):
@@ -68,22 +75,57 @@
     return total
 
 
-def load_kernel(values_hbm, values, sem):
+def prepare_kernel(meta, entries, values_hbm, values, table, sem):
     move = pltpu.make_async_copy(values_hbm, values, sem)
     move.start()
+    slots = values.shape[0]
+    count = meta[0]
+
+    def body(i, own):
+        for u in range(PREPARE):
+            k = i * PREPARE + u
+            entry = entries[k]
+            used = k < count
+            mine = entry >> OWN_BIT
+            at = jnp.where(mine == 1, own, count - 1 - (k - own))
+            table[jnp.where(used, at, slots + u)] = entry
+            own = own + jnp.where(used, mine, 0)
+        return own
+
+    steps = (count + PREPARE - 1) // PREPARE
+    table[slots + PREPARE] = lax.fori_loop(0, steps, body, jnp.int32(0))
     move.wait()
 
 
-def each_tile(count, step):
+def each_tile(meta, table, slots, owned, product, place, total):
+    own = table[slots + PREPARE]
+    low, high = (0, own) if owned else (own, meta[0])
+    dump = total.shape[0] - 1
+
     def body(i, _):
-        step(i * UNROLL)
+        first = low + i * UNROLL
+        entries = [table[jnp.minimum(first + u, high - 1)] for u in range(UNROLL)]
+        products = [product(entry) for entry in entries]
+        for u in range(UNROLL):
+            total[jnp.where(first + u < high, place(entries[u]), dump)] += products[u]
         return 0
 
-    lax.fori_loop(0, (count + UNROLL - 1) // UNROLL, body, 0)
-
-
-def forward_kernel(meta, rows, places, values, both, z1, z2, z3, o3, keep, send,
-                   block, total, block_sems):
+    lax.fori_loop(0, (high - low + UNROLL - 1) // UNROLL, body, 0)
+
+
+def forward_part(owned, meta, table, values, block, out, total):
+    slots, tile = values.shape[:2]
+
+    def product(entry):
+        features = block[field(entry, BLOCK_BITS)]
+        return jnp.dot(values[field(entry, SLOT_BITS)], features, preferred_element_type=F32)
+
+    each_tile(meta, table, slots, owned, product, lambda entry: field(entry, ROW_BITS), total)
+    for t in range(total.shape[0] - 1):
+        out[t * tile:(t + 1) * tile] = total[t].astype(BF16)
+
+
+def forward_send_kernel(meta, table, values, both, z1, z2, z3, o3, send, block, total, block_sems):
     q = z3.shape[0]
     moves = [(both, 0), (z1, 2 * q), (z2, 4 * q), (z3, 6 * q), (o3, 7 * q)]
     moves = [
@@ -95,26 +137,12 @@
     total[...] = jnp.zeros_like(total)
     for move in moves:
         move.wait()
-    count = meta[0]
-    core = meta[1]
-    dump = total.shape[0] - 1
-
-    def step(first):
-        products = [
-            jnp.dot(values[first + u], block[places[first + u]], preferred_element_type=F32)
-            for u in range(UNROLL)
-        ]
-        for u in range(UNROLL):
-            row = jnp.where(first + u < count, rows[first + u], dump)
-            total[row] += products[u]
-
-    each_tile(count, step)
-    tile = total.shape[1]
-    for p in range(N_PAIR):
-        for i in range(2):
-            at = pl.ds((2 * p + i) * tile, tile)
-            keep[at] = total[(2 * p + core) * 2 + i].astype(BF16)
-            send[at] = total[(2 * p + 1 - core) * 2 + i].astype(BF16)
+    forward_part(False, meta, table, values, block, send, total)
+
+
+def forward_keep_kernel(meta, table, values, block, keep, total):
+    total[...] = jnp.zeros_like(total)
+    forward_part(True, meta, table, values, block, keep, total)
 
 
 def middle_kernel(parts, weight, cotangent, activations, payload):
@@ -142,35 +170,27 @@
         payload[p, 2 * width:] = local[k:k + share, p // half * width:(p // half + 1) * width]
 
 
-def backward_kernel(meta, cols, places, values, mine, other, keep_far, keep_own, send_far, send_own,
-                    block, total, block_sems):
-    pairs, two = block.shape[1], block.shape[2]
-    moves = [
-        pltpu.make_async_copy(src.at[:, pl.ds(0, two)], block.at[i], block_sems.at[i])
-        for i, src in enumerate((mine, other))
-    ]
-    for move in moves:
-        move.start()
+def backward_part(owned, meta, table, values, back, total):
+    slots, tile = values.shape[:2]
+
+    def product(entry):
+        at = field(entry, ROW_BITS)
+        part = back[at >> 1, pl.ds((at & 1) * tile, tile)]
+        return jnp.dot(part, values[field(entry, SLOT_BITS)], preferred_element_type=F32)
+
+    each_tile(meta, table, slots, owned, product, lambda entry: field(entry, COL_BITS), total)
+
+
+def backward_own_kernel(meta, table, values, mine, total):
     total[...] = jnp.zeros_like(total)
-    for move in moves:
-        move.wait()
-    count = meta[0]
-    my_y = meta[2]
-    my_zl = meta[3]
-    dump = total.shape[0] - 1
-    tile = total.shape[1]
-
-    def step(first):
-        products = []
-        for u in range(UNROLL):
-            at = places[first + u]
-            back = block[at // (2 * pairs), at // 2 % pairs, pl.ds(at % 2 * tile, tile)]
-            products.append(jnp.dot(back, values[first + u], preferred_element_type=F32))
-        for u in range(UNROLL):
-            col = jnp.where(first + u < count, cols[first + u], dump)
-            total[col] += products[u]
-
-    each_tile(count, step)
+    backward_part(True, meta, table, values, mine, total)
+
+
+def backward_other_kernel(meta, table, values, other, owned, keep_far, keep_own, send_far, send_own,
+                          total):
+    total[...] = owned[...]
+    backward_part(False, meta, table, values, other, total)
+    my_y, my_zl, tile = meta[2], meta[3], total.shape[1]
     classes = (
         (0, keep_own, send_own, 0),
         (1, keep_far, send_far, 0),
@@ -196,27 +216,28 @@
     r = lax.axis_index("row")
     c = lax.axis_index("col")
     my_y, my_zl, core = r // N_Z, r % N_ZL, c % N_CORE
+    meta = jnp.stack([tile_count[0, 0], core, my_y, my_zl]).astype(jnp.int32)
+    rows, cols = tile_rows[0, 0], tile_cols[0, 0]
+    node = cols >> 1
+    distance = (node - my_zl) & (N_ZL - 1)
+    distance = jnp.where(distance == 0, 0, jnp.where(distance == 3, 1, distance + 1))
+    place = (distance * N_Y + ((node // N_Z) ^ my_y)) * N_ZH + ((node // N_ZL) & (N_ZH - 1))
+    entries = jnp.arange(slots, dtype=jnp.int32) | (((rows >> 2) * 2 + (rows & 1)) << ROW_BITS[0])
+    entries = entries | ((place * 2 + (cols & 1)) << BLOCK_BITS[0]) | (cols << COL_BITS[0])
+    entries = entries | ((((rows >> 1) & 1) == core).astype(jnp.int32) << OWN_BIT)
     params = pltpu.CompilerParams(vmem_limit_bytes=VMEM_LIMIT)
-    values = pl.pallas_call(
-        load_kernel,
-        out_shape=jax.ShapeDtypeStruct(tile_values.shape[2:], BF16),
-        in_specs=[ANY],
-        out_specs=VMEM,
+    values, table = pl.pallas_call(
+        prepare_kernel,
+        out_shape=(
+            jax.ShapeDtypeStruct(tile_values.shape[2:], BF16),
+            jax.ShapeDtypeStruct((slots + 2 * PREPARE,), jnp.int32),
+        ),
+        in_specs=[SMEM, SMEM, ANY],
+        out_specs=(VMEM, SMEM),
         scratch_shapes=[pltpu.SemaphoreType.DMA],
         compiler_params=params,
-        name="load_tiles",
-    )(tile_values[0, 0])
-    rows = tile_rows[0, 0]
-    cols = tile_cols[0, 0]
-    meta = jnp.stack([tile_count[0, 0], core, my_y, my_zl]).astype(jnp.int32)
-
-    at = cols // 2
-    distance = jnp.array([0, 2, 3, 1], jnp.int32)[(at - my_zl) % N_ZL]
-    col_places = (
-        (distance * N_Y + ((at // N_Z) ^ my_y)) * N_ZH + at // N_ZL % N_ZH
-    ) * 2 + cols % 2
-    at = rows // 2
-    row_places = (((at % N_CORE) ^ core) * N_PAIR + at // N_CORE) * 2 + rows % 2
+        name="prepare",
+    )(meta, entries, tile_values[0, 0])
 
     z0 = lax.all_gather(features[0, 0], "row", axis=0, tiled=True, axis_index_groups=ZH_GROUPS)
     o0 = shift(z0, 1, 0)
@@ -230,21 +251,31 @@
     half_rows = jax.ShapeDtypeStruct((n_col * sub // 2, width), BF16)
     one = jax.ShapeDtypeStruct((N_ZH * sub, width), BF16)
     three = jax.ShapeDtypeStruct((3 * N_ZH * sub, width), BF16)
-    flops = 2 * slots * tile * tile * width
-    keep, send = pl.pallas_call(
-        forward_kernel,
-        out_shape=(half_rows, half_rows),
-        in_specs=[SMEM, SMEM, SMEM, VMEM] + [ANY] * len(pieces),
+    all_cols = (cols_n + 1, tile, width)
+    cost = pl.CostEstimate(flops=slots * tile * tile * width, bytes_accessed=7 << 20, transcendentals=0)
+    send, block = pl.pallas_call(
+        forward_send_kernel,
+        out_shape=(half_rows, jax.ShapeDtypeStruct((cols_n, tile, width), BF16)),
+        in_specs=[SMEM, SMEM, VMEM] + [ANY] * len(pieces),
         out_specs=(VMEM, VMEM),
         scratch_shapes=[
-            pltpu.VMEM((cols_n, tile, width), BF16),
-            pltpu.VMEM((rows_n + 1, tile, width), F32),
+            pltpu.VMEM((rows_n // 2 + 1, tile, width), F32),
             pltpu.SemaphoreType.DMA((len(pieces),)),
         ],
         compiler_params=params,
-        cost_estimate=pl.CostEstimate(flops=flops, bytes_accessed=7 << 20, transcendentals=0),
-        name="forward_tiles",
-    )(meta, rows, col_places, values, *pieces)
+        cost_estimate=cost,
+        name="forward_send",
+    )(meta, table, values, *pieces)
+    keep = pl.pallas_call(
+        forward_keep_kernel,
+        out_shape=half_rows,
+        in_specs=[SMEM, SMEM, VMEM, VMEM],
+        out_specs=VMEM,
+        scratch_shapes=[pltpu.VMEM((rows_n // 2 + 1, tile, width), F32)],
+        compiler_params=params,
+        cost_estimate=cost,
+        name="forward_keep",
+    )(meta, table, values, block)
 
     both = (keep.astype(F32) + swap_cores(send).astype(F32)).astype(BF16)
     parts = exchange(both, "col", PAIR_GROUPS).reshape(N_PAIR, sub, width)
@@ -263,20 +294,25 @@
 
     mine = exchange(payload.reshape(-1, width), "col", PAIR_GROUPS).reshape(payload.shape)
     other = swap_cores(mine)
+    owned = pl.pallas_call(
+        backward_own_kernel,
+        out_shape=jax.ShapeDtypeStruct(all_cols, F32),
+        in_specs=[SMEM, SMEM, VMEM, VMEM],
+        out_specs=VMEM,
+        compiler_params=params,
+        cost_estimate=cost,
+        name="backward_own",
+    )(meta, table, values, mine)
     keep_far, keep_own, send_far, send_own = pl.pallas_call(
-        backward_kernel,
+        backward_other_kernel,
         out_shape=(three, one) * 2,
-        in_specs=[SMEM, SMEM, SMEM, VMEM] + [ANY] * 2,
+        in_specs=[SMEM, SMEM, VMEM, VMEM, VMEM],
         out_specs=(VMEM,) * 4,
-        scratch_shapes=[
-            pltpu.VMEM((N_CORE, N_PAIR, sub, width), BF16),
-            pltpu.VMEM((cols_n + 1, tile, width), F32),
-            pltpu.SemaphoreType.DMA((N_CORE,)),
-        ],
-        compiler_params=params,
-        cost_estimate=pl.CostEstimate(flops=flops, bytes_accessed=7 << 20, transcendentals=0),
-        name="backward_tiles",
-    )(meta, cols, row_places, values, mine, other)
+        scratch_shapes=[pltpu.VMEM(all_cols, F32)],
+        compiler_params=params,
+        cost_estimate=cost,
+        name="backward_other",
+    )(meta, table, values, other, owned)
 
     shared = add_up([mine[p, sub:] for p in range(N_PAIR)]) + add_up(
         [other[p, sub:] for p in range(N_PAIR)]

time: 171 us -> 169 us (0.988)
  waiting for transfers between devices: 34.4 us -> 31.1 us
  Pallas kernels: 5.53 us -> 7.92 us
    ppermute x2, waiting for transfers between devices: 3.82 us -> 1.31 us  [swap_cores(): return lax.ppermute(x, 'col', [(c, c ^ 1) for c in range(N_PAIR * N_CORE)])]
    pallas_call x3 -> x5, Pallas kernels: 4.65 us -> 7.04 us  [the longest x1 1.64 us: on_device(): pl.pallas_call(prepare_kernel, out_shape=(jax.ShapeDtypeStruct(tile_value...]
  transfers between devices with their start and end apart: 14 -> 14, of which waited for: 8 -> 8; matrix products, arithmetic and copies ran while one was open for 1% -> 2% of each run, Pallas kernels for 0% -> 2%
where the time goes in v4:
time: 169 us; the launch traced here: 168 us
  blocking collectives  70.7 us (42%)
  starting transfers between devices  50.1 us (30%)
  waiting for transfers between devices  31.1 us (18%)
  Pallas kernels  7.92 us (5%)
  local copies, waits for them, and re-layouts  4.55 us (3%)
  other arithmetic  2.13 us (1%)
    all_to_all x3, blocking collectives, exchange(): return lax.all_to_all(x, axis, 0, 0, tiled=True, axis_index_groups=groups)  44.5 us
    all_gather x1, blocking collectives, on_device(): lax.all_gather(features[0, 0], 'row', axis=0, tiled=True, axis_index_grou...  26.2 us
    ppermute x8, starting transfers between devices, shift(): return lax.ppermute(x, 'row', pairs)  21.4 us
    all_to_all x2, waiting for transfers between devices, exchange(): return lax.all_to_all(x, axis, 0, 0, tiled=True, axis_index_groups=groups)  16.7 us
    all_to_all x2, starting transfers between devices, exchange(): return lax.all_to_all(x, axis, 0, 0, tiled=True, axis_index_groups=groups)  15.8 us
    ppermute x8, waiting for transfers between devices, shift(): return lax.ppermute(x, 'row', pairs)  10.4 us
    ppermute x2, starting transfers between devices, two_along_z(): return lax.ppermute(x, ('row', 'col'), pairs)  9.05 us
    ppermute x2, starting transfers between devices, swap_cores(): return lax.ppermute(x, 'col', [(c, c ^ 1) for c in range(N_PAIR * N_CORE)])  3.83 us
  transfers between devices with their start and end apart: 14, of which 8 were waited for; matrix products, arithmetic and copies ran while one was open for 2% of the time, Pallas kernels for 2%

profile of v4, /device:TPU:32, one launch (start us, length us, event | category | flops | bytes accessed | tf_op | source)
XLA Modules:
  0.0 168.0 jit_solution(6451715694097220301)
XLA Ops:
  0.6 26.2 %all-gather = bf16[1,1,1024,128]{3,2,1,0:T(8,128)(2,1)S(1)} all-gather(bf16[1,1,256,128]{3,2,1,0:T(8,128)(2,1)} %param.7), channel_id=2, replica_groups={{0,64,128,192},{16,80,144,208},{32,96,160,224},{48,112,176,240},{256,32..., dimensions={2}, use_global_device_ids=true | all-gather | bytes 327680 | tf_op jit(solution)/shard_map/all_gather | solution.py:242
  26.8 3.5 %collective-permute-start = (bf16[1024,128]{1,0:T(8,128)(2,1)S(1)}, bf16[1024,128]{1,0:T(8,128)(2,1)S(1)}, u32[]{:S(2)}, u32[]{:S(2)}) collective-permute-start(bf16[1024,128]{1,0:T(8,128)(2,1)S(1)} %bitcast.75), channel_id=1, source_target_pairs={{0,256},{16,272},{32,288},{48,304},{64,320},{80,336},{96,352},{112... | collective-permute-start | bytes 786440 | tf_op jit(solution)/shard_map/ppermute | solution.py:34
  30.3 4.4 %collective-permute-start.3 = (bf16[1024,128]{1,0:T(8,128)(2,1)S(1)}, bf16[1024,128]{1,0:T(8,128)(2,1)S(1)}, u32[]{:S(2)}, u32[]{:S(2)}) collective-permute-start(bf16[1024,128]{1,0:T(8,128)(2,1)S(1)} %bitcast.76), channel_id=1, source_target_pairs={{0,224},{1,33},{2,226},{3,35},{4,228},{5,37},{6,230},{7,39},{8,232... | collective-permute-start | bytes 786440 | tf_op jit(solution)/shard_map/ppermute | solution.py:44
  34.7 0.3 collective-permute-done
  35.1 2.9 %collective-permute-start.2 = (bf16[2048,128]{1,0:T(8,128)(2,1)S(1)}, bf16[2048,128]{1,0:T(8,128)(2,1)S(1)}, u32[]{:S(2)}, u32[]{:S(2)}) collective-permute-start(bf16[2048,128]{1,0:T(8,128)(2,1)S(1)} %pad_maximum_fusion), channel_id=1, source_target_pairs={{0,240},{16,0},{32,16},{48,32},{64,48},{80,64},{96,80},{112,96},{1... | collective-permute-start | bytes 1572872 | tf_op jit(solution)/shard_map/ppermute | solution.py:34
  38.1 2.9 %collective-permute-start.1 = (bf16[2048,128]{1,0:T(8,128)(2,1)S(1)}, bf16[2048,128]{1,0:T(8,128)(2,1)S(1)}, u32[]{:S(2)}, u32[]{:S(2)}) collective-permute-start(bf16[2048,128]{1,0:T(8,128)(2,1)S(1)} %pad_maximum_fusion), channel_id=1, source_target_pairs={{0,16},{16,32},{32,48},{48,64},{64,80},{80,96},{96,112},{112,128},... | collective-permute-start | bytes 1572872 | tf_op jit(solution)/shard_map/ppermute | solution.py:34
  41.7 2.7 %collective-permute-done.3 = bf16[1024,128]{1,0:T(8,128)(2,1)S(1)} collective-permute-done((bf16[1024,128]{1,0:T(8,128)(2,1)S(1)}, bf16[1024,128]{1,0:T(8,128)(2,1)S(1)}, u32[]{:S(2)}, u32[]{:S(2)}) %collective-permute-start.3) | collective-permute-done | bytes 262176 | tf_op jit(solution)/shard_map/ppermute | solution.py:44
  44.4 2.1 %collective-permute-start.4 = (bf16[1024,128]{1,0:T(8,128)(2,1)S(1)}, bf16[1024,128]{1,0:T(8,128)(2,1)S(1)}, u32[]{:S(2)}, u32[]{:S(2)}) collective-permute-start(bf16[1024,128]{1,0:T(8,128)(2,1)S(1)} %collective-permute-done.3), channel_id=1, source_target_pairs={{0,256},{16,272},{32,288},{48,304},{64,320},{80,336},{96,352},{112... | collective-permute-start | bytes 786440 | tf_op jit(solution)/shard_map/ppermute | solution.py:34
  46.5 0.1 pad_add_fusion.meta
  46.6 0.7 fusion.5.entries
  47.3 2.2 %copy-done = bf16[1,1,128,128,128]{4,3,2,1,0:T(8,128)(2,1)S(1)} copy-done((bf16[1,1,128,128,128]{4,3,2,1,0:T(8,128)(2,1)S(1)}, bf16[1,1,128,128,128]{4,3,2,1,0:T(8,128)(2,1)}, u32[]{:S(2)}) %copy-start) | copy-done | bytes 4194328
  49.5 1.6 prepare.1
  51.1 1.5 collective-permute-done.4
  52.6 0.1 collective-permute-done.2
  52.7 0.0 collective-permute-done.1
  52.7 1.4 forward_send.1
  54.1 1.9 %collective-permute-start.5 = (bf16[2048,128]{1,0:T(8,128)(2,1)S(1)}, bf16[2048,128]{1,0:T(8,128)(2,1)S(1)}, u32[]{:S(2)}, u32[]{:S(2)}) collective-permute-start(bf16[2048,128]{1,0:T(8,128)(2,1)S(1)} %get-tuple-element.22), channel_id=1, source_target_pairs={{0,1},{1,0},{2,3},{3,2},{4,5},{5,4},{6,7},{7,6},{8,9},{9,8},{10,11... | collective-permute-start | bytes 1572872 | tf_op jit(solution)/shard_map/ppermute | solution.py:48
  56.0 1.2 forward_keep.1
  57.2 0.0 copy-start.1
  57.2 0.0 copy-start.2
  57.2 0.7 collective-permute-done.5
  57.9 0.1 add_convert_fusion.1
  58.1 19.0 %all_to_all.36.parts = bf16[8,256,128]{2,1,0:T(8,128)(2,1)S(1)} all-to-all(bf16[8,256,128]{2,1,0:T(8,128)(2,1)S(1)} %bitcast.74), channel_id=1, replica_groups={{0,2,4,6,8,10,12,14},{1,3,5,7,9,11,13,15},{16,18,20,22,24,26,28,30},{17..., dimensions={0} | all-to-all | bytes 1048576 | tf_op jit(solution)/shard_map/all_to_all | solution.py:64
  77.1 0.9 layer.1
  78.0 14.9 %all_to_all.37.mine = bf16[8,288,128]{2,1,0:T(8,128)(2,1)S(1)} all-to-all(bf16[8,288,128]{2,1,0:T(8,128)(2,1)S(1)} %get-tuple-element.24), channel_id=1, replica_groups={{0,2,4,6,8,10,12,14},{1,3,5,7,9,11,13,15},{16,18,20,22,24,26,28,30},{17..., dimensions={0} | all-to-all | bytes 1179648 | tf_op jit(solution)/shard_map/all_to_all | solution.py:64
  92.9 1.9 %collective-permute-start.6 = (bf16[8,288,128]{2,1,0:T(8,128)(2,1)S(1)}, bf16[8,288,128]{2,1,0:T(8,128)(2,1)S(1)}, u32[]{:S(2)}, u32[]{:S(2)}) collective-permute-start(bf16[8,288,128]{2,1,0:T(8,128)(2,1)S(1)} %all_to_all.37.mine), channel_id=1, source_target_pairs={{0,1},{1,0},{2,3},{3,2},{4,5},{5,4},{6,7},{7,6},{8,9},{9,8},{10,11... | collective-permute-start | bytes 1769480 | tf_op jit(solution)/shard_map/ppermute | solution.py:48
  94.8 1.3 backward_own.1.owned
  96.1 0.6 collective-permute-done.6.other
  96.8 1.5 backward_other.1
  98.3 1.9 %collective-permute-start.7 = (bf16[3072,128]{1,0:T(8,128)(2,1)S(1)}, bf16[3072,128]{1,0:T(8,128)(2,1)S(1)}, u32[]{:S(2)}, u32[]{:S(2)}) collective-permute-start(bf16[3072,128]{1,0:T(8,128)(2,1)S(1)} %get-tuple-element.27), channel_id=1, source_target_pairs={{0,256},{16,272},{32,288},{48,304},{64,320},{80,336},{96,352},{112... | collective-permute-start | bytes 2359304 | tf_op jit(solution)/shard_map/ppermute | solution.py:34
  100.2 0.7 broadcast_in_dim.9
  100.9 9.0 %all-to-all-start.2 = ((bf16[16,32,128]{2,1,0:T(8,128)(2,1)}), bf16[16,32,128]{2,1,0:T(8,128)(2,1)S(1)}, u32[]{:S(2)}, u32[]{:S(2)}) async-start(bf16[16,32,128]{2,1,0:T(8,128)(2,1)} %broadcast_in_dim.9), calls=%async_computation.2 | async-start | bytes 262144 | tf_op jit(solution)/shard_map/all_to_all | solution.py:64
  109.9 2.3 %collective-permute-start.11 = (bf16[1024,128]{1,0:T(8,128)(2,1)S(1)}, bf16[1024,128]{1,0:T(8,128)(2,1)S(1)}, u32[]{:S(2)}, u32[]{:S(2)}) collective-permute-start(bf16[1024,128]{1,0:T(8,128)(2,1)S(1)} %get-tuple-element.31), channel_id=1, source_target_pairs={{0,256},{16,272},{32,288},{48,304},{64,320},{80,336},{96,352},{112... | collective-permute-start | bytes 786440 | tf_op jit(solution)/shard_map/ppermute | solution.py:34
  112.2 8.4 %collective-permute-done.7 = bf16[3072,128]{1,0:T(8,128)(2,1)S(1)} collective-permute-done((bf16[3072,128]{1,0:T(8,128)(2,1)S(1)}, bf16[3072,128]{1,0:T(8,128)(2,1)S(1)}, u32[]{:S(2)}, u32[]{:S(2)}) %collective-permute-start.7) | collective-permute-done | bytes 786464 | tf_op jit(solution)/shard_map/ppermute | solution.py:34
  120.6 0.2 add_convert_fusion
  120.8 0.1 fusion.9
  120.9 4.6 %collective-permute-start.10 = (bf16[1024,128]{1,0:T(8,128)(2,1)S(1)}, bf16[1024,128]{1,0:T(8,128)(2,1)S(1)}, u32[]{:S(2)}, u32[]{:S(2)}) collective-permute-start(bf16[1024,128]{1,0:T(8,128)(2,1)S(1)} %get-tuple-element.38), channel_id=1, source_target_pairs={{0,224},{1,33},{2,226},{3,35},{4,228},{5,37},{6,230},{7,39},{8,232... | collective-permute-start | bytes 786440 | tf_op jit(solution)/shard_map/ppermute | solution.py:44
  125.5 1.9 %collective-permute-start.9 = (bf16[1024,128]{1,0:T(8,128)(2,1)S(1)}, bf16[1024,128]{1,0:T(8,128)(2,1)S(1)}, u32[]{:S(2)}, u32[]{:S(2)}) collective-permute-start(bf16[1024,128]{1,0:T(8,128)(2,1)S(1)} %get-tuple-element.39), channel_id=1, source_target_pairs={{0,240},{16,0},{32,16},{48,32},{64,48},{80,64},{96,80},{112,96},{1... | collective-permute-start | bytes 786440 | tf_op jit(solution)/shard_map/ppermute | solution.py:34
  127.4 3.9 %collective-permute-start.8 = (bf16[1024,128]{1,0:T(8,128)(2,1)S(1)}, bf16[1024,128]{1,0:T(8,128)(2,1)S(1)}, u32[]{:S(2)}, u32[]{:S(2)}) collective-permute-start(bf16[1024,128]{1,0:T(8,128)(2,1)S(1)} %get-tuple-element.40), channel_id=1, source_target_pairs={{0,16},{16,32},{32,48},{48,64},{64,80},{80,96},{96,112},{112,128},... | collective-permute-start | bytes 786440 | tf_op jit(solution)/shard_map/ppermute | solution.py:34
  131.3 0.0 all-to-all-done.2
  131.4 10.6 %all_to_all.38 = bf16[16,32,128]{2,1,0:T(8,128)(2,1)S(1)} all-to-all(bf16[16,32,128]{2,1,0:T(8,128)(2,1)S(1)} %broadcast_in_dim.19), channel_id=1, replica_groups={{0,2,4,6,8,10,12,14,256,258,260,262,264,266,268,270},{1,3,5,7,9,11,13,1..., dimensions={0} | all-to-all | bytes 262144 | tf_op jit(solution)/shard_map/all_to_all | solution.py:64
  142.0 0.0 collective-permute-done.8
  142.0 0.9 add_convert_fusion.2
  142.9 6.8 %all-to-all-start.4 = ((bf16[4,256,128]{2,1,0:T(8,128)(2,1)}), bf16[4,256,128]{2,1,0:T(8,128)(2,1)S(1)}, u32[]{:S(2)}, u32[]{:S(2)}) async-start(bf16[4,256,128]{2,1,0:T(8,128)(2,1)} %bitcast.23), calls=%async_computation.4 | async-start | bytes 524288 | tf_op jit(solution)/shard_map/all_to_all | solution.py:64
  149.7 0.1 copy.12
  149.8 0.8 copy.14
  150.5 16.7 %all-to-all-done.4 = bf16[4,256,128]{2,1,0:T(8,128)(2,1)S(1)} async-done(((bf16[4,256,128]{2,1,0:T(8,128)(2,1)}), bf16[4,256,128]{2,1,0:T(8,128)(2,1)S(1)}, u32[]{:S(2)}, u32[]{:S(2)}) %all-to-all-start.4) | async-done | bytes 262176 | tf_op jit(solution)/shard_map/all_to_all | solution.py:64
  167.2 0.8 copy.13
  (12 shorter events, 0.2 us)
Async XLA Ops:
  26.8 8.3 %collective-permute-start = (bf16[1024,128]{1,0:T(8,128)(2,1)S(1)}, bf16[1024,128]{1,0:T(8,128)(2,1)S(1)}, u32[]{:S(2)}, u32[]{:S(2)}) collective-permute-start(bf16[1024,128]{1,0:T(8,128)(2,1)S(1)} %bitcast.75), channel_id=1, source_target_pairs={{0,256},{16,272},{32,288},{48,304},{64,320},{80,336},{96,352},{112... | collective-permute-start | bytes 786440 | tf_op jit(solution)/shard_map/ppermute | solution.py:34
  30.3 14.1 %collective-permute-start.3 = (bf16[1024,128]{1,0:T(8,128)(2,1)S(1)}, bf16[1024,128]{1,0:T(8,128)(2,1)S(1)}, u32[]{:S(2)}, u32[]{:S(2)}) collective-permute-start(bf16[1024,128]{1,0:T(8,128)(2,1)S(1)} %bitcast.76), channel_id=1, source_target_pairs={{0,224},{1,33},{2,226},{3,35},{4,228},{5,37},{6,230},{7,39},{8,232... | collective-permute-start | bytes 786440 | tf_op jit(solution)/shard_map/ppermute | solution.py:44
  35.1 17.6 %collective-permute-start.2 = (bf16[2048,128]{1,0:T(8,128)(2,1)S(1)}, bf16[2048,128]{1,0:T(8,128)(2,1)S(1)}, u32[]{:S(2)}, u32[]{:S(2)}) collective-permute-start(bf16[2048,128]{1,0:T(8,128)(2,1)S(1)} %pad_maximum_fusion), channel_id=1, source_target_pairs={{0,240},{16,0},{32,16},{48,32},{64,48},{80,64},{96,80},{112,96},{1... | collective-permute-start | bytes 1572872 | tf_op jit(solution)/shard_map/ppermute | solution.py:34
  38.1 14.7 %collective-permute-start.1 = (bf16[2048,128]{1,0:T(8,128)(2,1)S(1)}, bf16[2048,128]{1,0:T(8,128)(2,1)S(1)}, u32[]{:S(2)}, u32[]{:S(2)}) collective-permute-start(bf16[2048,128]{1,0:T(8,128)(2,1)S(1)} %pad_maximum_fusion), channel_id=1, source_target_pairs={{0,16},{16,32},{32,48},{48,64},{64,80},{80,96},{96,112},{112,128},... | collective-permute-start | bytes 1572872 | tf_op jit(solution)/shard_map/ppermute | solution.py:34
  44.4 8.3 %collective-permute-start.4 = (bf16[1024,128]{1,0:T(8,128)(2,1)S(1)}, bf16[1024,128]{1,0:T(8,128)(2,1)S(1)}, u32[]{:S(2)}, u32[]{:S(2)}) collective-permute-start(bf16[1024,128]{1,0:T(8,128)(2,1)S(1)} %collective-permute-done.3), channel_id=1, source_target_pairs={{0,256},{16,272},{32,288},{48,304},{64,320},{80,336},{96,352},{112... | collective-permute-start | bytes 786440 | tf_op jit(solution)/shard_map/ppermute | solution.py:34
  47.3 2.2 %copy-start = (bf16[1,1,128,128,128]{4,3,2,1,0:T(8,128)(2,1)S(1)}, bf16[1,1,128,128,128]{4,3,2,1,0:T(8,128)(2,1)}, u32[]{:S(2)}) copy-start(bf16[1,1,128,128,128]{4,3,2,1,0:T(8,128)(2,1)} %param.9) | copy-start | bytes 12582916
  54.1 3.8 %collective-permute-start.5 = (bf16[2048,128]{1,0:T(8,128)(2,1)S(1)}, bf16[2048,128]{1,0:T(8,128)(2,1)S(1)}, u32[]{:S(2)}, u32[]{:S(2)}) collective-permute-start(bf16[2048,128]{1,0:T(8,128)(2,1)S(1)} %get-tuple-element.22), channel_id=1, source_target_pairs={{0,1},{1,0},{2,3},{3,2},{4,5},{5,4},{6,7},{7,6},{8,9},{9,8},{10,11... | collective-permute-start | bytes 1572872 | tf_op jit(solution)/shard_map/ppermute | solution.py:48
  57.2 19.9 %copy-start.1 = (bf16[256,256]{1,0:T(8,128)(2,1)S(1)}, bf16[256,256]{1,0:T(8,128)(2,1)}, u32[]{:S(2)}) copy-start(bf16[256,256]{1,0:T(8,128)(2,1)} %cotangent.1) | copy-start | bytes 393220
  57.2 19.9 %copy-start.2 = (bf16[128,256]{1,0:T(8,128)(2,1)S(1)}, bf16[128,256]{1,0:T(8,128)(2,1)}, u32[]{:S(2)}) copy-start(bf16[128,256]{1,0:T(8,128)(2,1)} %weight.1) | copy-start | bytes 196612
  92.9 3.9 %collective-permute-start.6 = (bf16[8,288,128]{2,1,0:T(8,128)(2,1)S(1)}, bf16[8,288,128]{2,1,0:T(8,128)(2,1)S(1)}, u32[]{:S(2)}, u32[]{:S(2)}) collective-permute-start(bf16[8,288,128]{2,1,0:T(8,128)(2,1)S(1)} %all_to_all.37.mine), channel_id=1, source_target_pairs={{0,1},{1,0},{2,3},{3,2},{4,5},{5,4},{6,7},{7,6},{8,9},{9,8},{10,11... | collective-permute-start | bytes 1769480 | tf_op jit(solution)/shard_map/ppermute | solution.py:48
  98.3 22.3 %collective-permute-start.7 = (bf16[3072,128]{1,0:T(8,128)(2,1)S(1)}, bf16[3072,128]{1,0:T(8,128)(2,1)S(1)}, u32[]{:S(2)}, u32[]{:S(2)}) collective-permute-start(bf16[3072,128]{1,0:T(8,128)(2,1)S(1)} %get-tuple-element.27), channel_id=1, source_target_pairs={{0,256},{16,272},{32,288},{48,304},{64,320},{80,336},{96,352},{112... | collective-permute-start | bytes 2359304 | tf_op jit(solution)/shard_map/ppermute | solution.py:34
  100.9 30.4 %all-to-all-start.2 = ((bf16[16,32,128]{2,1,0:T(8,128)(2,1)}), bf16[16,32,128]{2,1,0:T(8,128)(2,1)S(1)}, u32[]{:S(2)}, u32[]{:S(2)}) async-start(bf16[16,32,128]{2,1,0:T(8,128)(2,1)} %broadcast_in_dim.9), calls=%async_computation.2 | async-start | bytes 262144 | tf_op jit(solution)/shard_map/all_to_all | solution.py:64
  109.9 32.1 %collective-permute-start.11 = (bf16[1024,128]{1,0:T(8,128)(2,1)S(1)}, bf16[1024,128]{1,0:T(8,128)(2,1)S(1)}, u32[]{:S(2)}, u32[]{:S(2)}) collective-permute-start(bf16[1024,128]{1,0:T(8,128)(2,1)S(1)} %get-tuple-element.31), channel_id=1, source_target_pairs={{0,256},{16,272},{32,288},{48,304},{64,320},{80,336},{96,352},{112... | collective-permute-start | bytes 786440 | tf_op jit(solution)/shard_map/ppermute | solution.py:34
  120.9 21.1 %collective-permute-start.10 = (bf16[1024,128]{1,0:T(8,128)(2,1)S(1)}, bf16[1024,128]{1,0:T(8,128)(2,1)S(1)}, u32[]{:S(2)}, u32[]{:S(2)}) collective-permute-start(bf16[1024,128]{1,0:T(8,128)(2,1)S(1)} %get-tuple-element.38), channel_id=1, source_target_pairs={{0,224},{1,33},{2,226},{3,35},{4,228},{5,37},{6,230},{7,39},{8,232... | collective-permute-start | bytes 786440 | tf_op jit(solution)/shard_map/ppermute | solution.py:44
  125.5 16.5 %collective-permute-start.9 = (bf16[1024,128]{1,0:T(8,128)(2,1)S(1)}, bf16[1024,128]{1,0:T(8,128)(2,1)S(1)}, u32[]{:S(2)}, u32[]{:S(2)}) collective-permute-start(bf16[1024,128]{1,0:T(8,128)(2,1)S(1)} %get-tuple-element.39), channel_id=1, source_target_pairs={{0,240},{16,0},{32,16},{48,32},{64,48},{80,64},{96,80},{112,96},{1... | collective-permute-start | bytes 786440 | tf_op jit(solution)/shard_map/ppermute | solution.py:34
  127.4 14.6 %collective-permute-start.8 = (bf16[1024,128]{1,0:T(8,128)(2,1)S(1)}, bf16[1024,128]{1,0:T(8,128)(2,1)S(1)}, u32[]{:S(2)}, u32[]{:S(2)}) collective-permute-start(bf16[1024,128]{1,0:T(8,128)(2,1)S(1)} %get-tuple-element.40), channel_id=1, source_target_pairs={{0,16},{16,32},{32,48},{48,64},{64,80},{80,96},{96,112},{112,128},... | collective-permute-start | bytes 786440 | tf_op jit(solution)/shard_map/ppermute | solution.py:34
  142.9 24.3 %all-to-all-start.4 = ((bf16[4,256,128]{2,1,0:T(8,128)(2,1)}), bf16[4,256,128]{2,1,0:T(8,128)(2,1)S(1)}, u32[]{:S(2)}, u32[]{:S(2)}) async-start(bf16[4,256,128]{2,1,0:T(8,128)(2,1)} %bitcast.23), calls=%async_computation.4 | async-start | bytes 524288 | tf_op jit(solution)/shard_map/all_to_all | solution.py:64
